TPU v7x, 512 devices: a whole 4x4x16 slice. The times are simulated.
512 devices in a mesh: tok: 32 (over z, core), col: 16 (over x, y).
Axes of the slice: x: 4, y: 4, z: 16, core: 2. Of those that a mesh axis runs over, the one named last changes fastest.
Arguments:
- tokens: bfloat16 [24576, 2048], P('tok', 'col'), may hold values from -6 to 6
- cotangent: bfloat16 [24576, 2048], P('tok', 'col'), may hold values from -6 to 6
- query_weight: bfloat16 [2048, 2048], P(None, 'col'), may hold values from -1 to 1
- slot_keys: bfloat16 [32768, 2048], P('tok', 'col'), may hold values from -64 to 64
- values: float32 [32768, 2048], P('tok', 'col'), may hold values from -6 to 6
- momentum: float32 [32768, 2048], P('tok', 'col'), may hold values from -0.3 to 0.3
- page_ids: int32 [384, 4], P('tok'), may hold values from 0 to 255, as said below
- last_step: int32 [256], P('tok'), may hold values from 0 to 63
- decay_rate: float32 [2048], P('col'), may hold values from 0.004 to 0.08
- gate_weight: bfloat16 [2048, 2048], P(None, 'col'), may hold values from -0.125 to 0.125
- out_weight: bfloat16 [2048, 2048], P('col'), may hold values from -0.1875 to 0.1875
Outputs:
- layer_out: bfloat16 [24576, 2048], P('tok', 'col')
- new_values: float32 [32768, 2048], P('tok', 'col')
- new_momentum: float32 [32768, 2048], P('tok', 'col')
Inputs may be any that keep to these rules, and one draw needn't show every extreme that they name: `page_ids`: page p belongs to owner group p // 8. Among the 48 pages listed by the blocks of one index of tok, counted with repeats, at most 2 belong to any one owner group, and one owner group gets exactly 2 from every index of tok. A block may list a page more than once.
All inputs are finite; a program needn't handle non-finite values.
Results may differ from a plain program's by a relative error of at most 0.014.
Values may be sent and summed in bfloat16 or wider, within the bound.
A program may use at most 64 MiB of HBM per device.

v0:
```python
import jax
import jax.numpy as jnp
from jax import lax
from jax.sharding import PartitionSpec as P

KW = 2048
STEP = 64


MOMENTUM_RATE = 0.9
LEARN_RATE = 1.0


def side_by_side(arrays, axis, dim, along):
    ends, at = ([], 0)
    for a in arrays[:-1]:
        at += a.shape[along]
        ends.append(at)
    both = jnp.concatenate(arrays, axis=along)
    return tuple(jnp.split(lax.all_gather(both, axis, axis=dim, tiled=True), ends, axis=along))


def split_up(shard, dim, count):
    before, after = (shard.shape[:dim], shard.shape[dim + 1 :])
    return jnp.moveaxis(shard.reshape(*before, count, -1, *after), dim, 0)


def sum_at_owner(shard, axis, dim):
    count = lax.axis_size(axis)
    pieces = lax.all_to_all(split_up(shard, dim, count), axis, 0, 0, tiled=True)
    return jnp.sum(pieces, axis=0)


def joined_along(pieces, dim):
    shape = list(pieces.shape[1:])
    shape[dim] *= pieces.shape[0]
    return jnp.moveaxis(pieces, 0, dim).reshape(shape)


def from_everyone(shard, axis):
    count = lax.axis_size(axis)
    return lax.all_to_all(
        jnp.broadcast_to(shard[None], (count, *shard.shape)), axis, 0, 0, tiled=True
    )


def collect(shard, axis, dim):
    return joined_along(from_everyone(shard, axis), dim)


def summed_on_arrival(shard, axis, dim):
    pieces = split_up(shard, dim, lax.axis_size(axis))
    arrived = lax.all_to_all(pieces, axis, split_axis=0, concat_axis=0, tiled=True)
    return arrived.astype(jnp.float32).sum(axis=0)


def per_device(
    tokens,
    cotangent,
    query_weight,
    slot_keys,
    values,
    momentum,
    page_ids,
    last_step,
    decay_rate,
    gate_weight,
    out_weight,
):
    tok_rows = tokens.shape[0]
    col_width = values.shape[1]
    key_width = slot_keys.shape[1]
    block_count, per_block = page_ids.shape
    block_rows = tok_rows // block_count
    pages_local = last_step.shape[0]
    page_slots = values.shape[0] // pages_local
    owners = lax.axis_size("tok")
    capacity = max(2, per_block * block_count // owners + 1)
    send_slots = owners * capacity
    listed_slots = per_block * page_slots
    elapsed = (STEP - last_step).astype(jnp.float32)
    factor = jnp.exp(-elapsed[:, None] * decay_rate[None, :])
    stored = values.reshape(pages_local, page_slots, col_width)
    decayed = (stored * factor[:, None, :]).astype(jnp.bfloat16)
    key_pages = slot_keys.reshape(pages_local, page_slots, key_width)
    token_piece, cotangent_piece = side_by_side((tokens, cotangent), "col", 1, 0)
    query_sum = jnp.dot(token_piece, query_weight, preferred_element_type=jnp.float32)
    gate_logits = jnp.dot(token_piece, gate_weight, preferred_element_type=jnp.float32)
    grad_gated = jnp.einsum(
        "nd,cd->nc", cotangent_piece, out_weight, preferred_element_type=jnp.float32
    )
    requested = page_ids.reshape(-1)
    page_owner = requested // pages_local
    local_page = requested % pages_local
    request_count = requested.shape[0]
    positions = jnp.arange(request_count)
    same_owner = page_owner[:, None] == page_owner[None, :]
    slot_rank = jnp.sum(same_owner & (positions[None, :] < positions[:, None]), axis=1)
    send_slot = page_owner * capacity + slot_rank
    slot_match = send_slot[:, None] == jnp.arange(send_slots)[None, :]
    wanted = jnp.sum(jnp.where(slot_match, local_page[:, None] + 1, 0), axis=0) - 1
    wanted = wanted.reshape(owners, capacity)
    incoming = lax.all_to_all(wanted, "tok", split_axis=0, concat_axis=0, tiled=True)
    occupied = (incoming >= 0)[:, :, None, None]
    chosen = jnp.clip(incoming, 0, pages_local - 1)
    reply_keys = jnp.where(occupied, key_pages[chosen], jnp.zeros((), jnp.bfloat16))
    reply_values = jnp.where(occupied, decayed[chosen], jnp.zeros((), jnp.bfloat16))
    got_keys = lax.all_to_all(reply_keys, "tok", split_axis=0, concat_axis=0, tiled=True)
    got_values = lax.all_to_all(reply_values, "tok", split_axis=0, concat_axis=0, tiled=True)
    block_keys = got_keys.reshape(send_slots, page_slots, key_width)[send_slot]
    block_keys = block_keys.reshape(block_count, listed_slots, key_width)
    block_values = got_values.reshape(send_slots, page_slots, col_width)[send_slot]
    block_values = block_values.reshape(block_count, listed_slots, col_width)
    queries = query_sum.astype(jnp.bfloat16).reshape(block_count, block_rows, key_width)
    partial_scores = jnp.einsum(
        "bnk,bsk->bns", queries, block_keys, preferred_element_type=jnp.float32
    )
    score_scale = KW ** (-0.5)
    flat_scores = partial_scores.reshape(tok_rows, listed_slots)
    score_share = sum_at_owner(flat_scores, "col", 0) * score_scale
    share_weights = jax.nn.softmax(score_share, axis=-1).astype(jnp.bfloat16)
    weights = collect(share_weights, "col", 0).reshape(block_count, block_rows, listed_slots)
    memory = jnp.einsum("bns,bsd->bnd", weights, block_values, preferred_element_type=jnp.float32)
    memory = memory.reshape(tok_rows, col_width)
    activation = jax.nn.silu(gate_logits)
    gated_memory = (memory * activation).astype(jnp.bfloat16)
    out_terms = jnp.dot(gated_memory, out_weight, preferred_element_type=jnp.float32)
    layer_out = summed_on_arrival(out_terms.astype(jnp.bfloat16), "col", 1).astype(jnp.bfloat16)
    grad_memory = (
        (grad_gated * activation).astype(jnp.bfloat16).reshape(block_count, block_rows, col_width)
    )
    slot_grads = jnp.einsum(
        "bns,bnd->bsd", weights, grad_memory, preferred_element_type=jnp.float32
    ).astype(jnp.bfloat16)
    outgoing = jnp.zeros((send_slots, page_slots, col_width), jnp.bfloat16)
    outgoing = outgoing.at[send_slot].set(slot_grads.reshape(request_count, page_slots, col_width))
    returned = lax.all_to_all(
        outgoing.reshape(owners, capacity, page_slots, col_width),
        "tok",
        split_axis=0,
        concat_axis=0,
        tiled=True,
    )
    page_match = incoming.reshape(1, send_slots) == jnp.arange(pages_local)[:, None]
    page_grad = jnp.dot(
        page_match.astype(jnp.bfloat16),
        returned.reshape(send_slots, page_slots * col_width),
        preferred_element_type=jnp.float32,
    )
    page_grad = page_grad.reshape(pages_local, page_slots, col_width)
    touched = jnp.any(page_match, axis=1)[:, None, None]
    moment = momentum.reshape(pages_local, page_slots, col_width)
    new_momentum = jnp.where(
        touched, MOMENTUM_RATE * moment + page_grad * factor[:, None, :], moment
    )
    new_values = jnp.where(touched, stored * factor[:, None, :] - LEARN_RATE * new_momentum, stored)
    return (layer_out, new_values.reshape(-1, col_width), new_momentum.reshape(-1, col_width))


def solution(mesh):
    in_specs = (
        P("tok", "col"),
        P("tok", "col"),
        P(None, "col"),
        P("tok", "col"),
        P("tok", "col"),
        P("tok", "col"),
        P("tok", None),
        P("tok"),
        P("col"),
        P(None, "col"),
        P("col", None),
    )
    out_specs = (P("tok", "col"), P("tok", "col"), P("tok", "col"))
    return jax.shard_map(
        per_device, mesh=mesh, in_specs=in_specs, out_specs=out_specs, check_vma=False
    )
```

profile of v0, /device:TPU:1, one launch (start us, length us, event | category | flops | bytes accessed | tf_op | source)
XLA Modules:
  0.0 485.4 jit_solution(6944364220590744377)
XLA Ops:
  7.2 1.9 pad_maximum_fusion
  9.1 0.8 copy.67
  10.0 0.2 convert_reduce_fusion
  10.2 0.1 select_reduce_fusion
  10.3 0.1 sub.34
  10.4 28.3 %all_to_all.36 = s32[32,1,2]{2,1,0:T(1,128)S(1)} all-to-all(s32[32,1,2]{2,1,0:T(1,128)S(1)} %bitcast.100), channel_id=1, replica_groups=mesh['tok'=32,'col'=16] {'tok'}, dimensions={0} | all-to-all | bytes 512 | tf_op jit(solution)/shard_map/all_to_all | solution.py:103
  38.8 0.1 copy.70
  39.0 0.1 reshape.344
  39.2 1.0 gather_fusion
  40.1 1.5 broadcast_select_fusion.1
  41.7 4.6 all-to-all-start.1
  46.4 99.2 %all-to-all-done.1 = bf16[32,2,128,128]{3,2,1,0:T(8,128)(2,1)S(1)} async-done(((bf16[32,2,128,128]{3,2,1,0:T(8,128)(2,1)}), bf16[32,2,128,128]{3,2,1,0:T(8,128)(2,1)S(1)}, u32[]{:S(2)}, u32[]{:S(2)}) %all-to-all-start.1) | async-done | bytes 2097184 | tf_op jit(solution)/shard_map/all_to_all | solution.py:108
  145.6 2.0 gather_fusion.1
  147.5 3.0 fusion.25
  150.5 0.7 fusion.40
  151.2 25.5 %all_to_all.37 = f32[16,48,512]{2,1,0:T(8,128)S(1)} all-to-all(f32[16,48,512]{2,1,0:T(8,128)S(1)} %bitcast.91), channel_id=1, replica_groups=mesh['tok'=32,'col'=16] {'col'}, dimensions={0} | all-to-all | bytes 3145728 | tf_op jit(solution)/shard_map/all_to_all | solution.py:30
  176.7 0.1 reduce_sum.53
  176.8 0.1 multiply_reduce_fusion
  176.9 0.2 fusion.32
  177.1 0.1 divide_convert_fusion
  177.3 1.0 broadcast_in_dim.44
  178.2 4.2 all-to-all-start.3
  182.4 2.9 divide_multiply_fusion
  185.3 0.7 copy-done.8
  186.0 2.9 fusion.22
  188.9 3.9 all-to-all-done.3
  192.8 0.6 convolution_convert_fusion.1
  193.5 1.9 broadcast_in_dim.76
  195.3 6.6 %scatter_fusion = bf16[64,128,128]{2,1,0:T(8,128)(2,1)} fusion(bf16[64,128,128]{2,1,0:T(8,128)(2,1)} %broadcast_in_dim.76, s32[48]{0:T(128)S(1)} %fusion.39, bf16[48,128,128]{2,1,0:T(8,128)(2,1)S(1)} %bitcast.90), kind=kCustom, calls=%fused_computation.4 | custom fusion | bytes 4718784 | tf_op jit(solution)/shard_map/scatter | solution.py:136
  202.0 10.9 %all-to-all-start.6 = ((bf16[32,2,128,128]{3,2,1,0:T(8,128)(2,1)}), bf16[32,2,128,128]{3,2,1,0:T(8,128)(2,1)S(1)}, u32[]{:S(2)}, u32[]{:S(2)}) async-start(bf16[32,2,128,128]{3,2,1,0:T(8,128)(2,1)} %bitcast.22), calls=%async_computation.6 | async-start | bytes 4194304 | tf_op jit(solution)/shard_map/all_to_all | solution.py:137
  213.0 0.5 broadcast.319
  213.5 0.7 reduce.4
  214.2 0.1 eq.49
  214.3 0.1 fusion.35
  214.5 97.1 %all-to-all-done.6 = bf16[32,2,128,128]{3,2,1,0:T(8,128)(2,1)S(1)} async-done(((bf16[32,2,128,128]{3,2,1,0:T(8,128)(2,1)}), bf16[32,2,128,128]{3,2,1,0:T(8,128)(2,1)S(1)}, u32[]{:S(2)}, u32[]{:S(2)}) %all-to-all-start.6) | async-done | bytes 2097184 | tf_op jit(solution)/shard_map/all_to_all | solution.py:137
  311.5 3.7 subtract_select_fusion
  315.3 1.0 gather_fusion.2
  316.3 0.2 broadcast_select_fusion
  316.5 105.6 %all_to_all.38 = bf16[32,2,128,128]{3,2,1,0:T(8,128)(2,1)S(1)} all-to-all(bf16[32,2,128,128]{3,2,1,0:T(8,128)(2,1)S(1)} %broadcast_select_fusion), channel_id=1, replica_groups=mesh['tok'=32,'col'=16] {'tok'}, dimensions={0} | all-to-all | bytes 4194304 | tf_op jit(solution)/shard_map/all_to_all | solution.py:109
  422.1 2.0 gather_fusion.3
  424.1 1.9 fusion.41
  426.0 1.0 fusion.9
  427.0 2.5 copy.109
  429.5 4.6 all-to-all-start.5
  434.1 0.9 copy.81
  435.0 0.9 copy.82
  435.9 39.6 %all-to-all-done.5 = bf16[16,768,128]{2,1,0:T(8,128)(2,1)} async-done(((bf16[16,768,128]{2,1,0:T(8,128)(2,1)}), bf16[16,768,128]{2,1,0:T(8,128)(2,1)}, u32[]{:S(2)}, u32[]{:S(2)}) %all-to-all-start.5) | async-done | bytes 3145760 | tf_op jit(solution)/shard_map/all_to_all | solution.py:53
  475.5 3.1 reduce_sum.55
  (46 shorter events, 0.7 us)
Async XLA Ops:
  7.2 178.9 %copy-start = (bf16[128,2048]{1,0:T(8,128)(2,1)S(1)}, bf16[128,2048]{1,0:T(8,128)(2,1)}, u32[]{:S(2)}) copy-start(bf16[128,2048]{1,0:T(8,128)(2,1)} %param.21) | copy-start | bytes 1572868
  7.2 32.0 %copy-start.1 = (bf16[1024,128]{1,0:T(8,128)(2,1)S(1)}, bf16[1024,128]{1,0:T(8,128)(2,1)}, u32[]{:S(2)}) copy-start(bf16[1024,128]{1,0:T(8,128)(2,1)} %param.14) | copy-start | bytes 786436
  7.2 140.3 %all-gather.2.cloned.1.call-start = ((), (), s32[]{:S(2)}) async-start(), calls=%async_computation.7 | async-start | bytes 6684672 | tf_op jit(solution)/shard_map/all_gather | solution.py:20
  41.7 103.9 %all-to-all-start.1 = ((bf16[32,2,128,128]{3,2,1,0:T(8,128)(2,1)}), bf16[32,2,128,128]{3,2,1,0:T(8,128)(2,1)S(1)}, u32[]{:S(2)}, u32[]{:S(2)}) async-start(bf16[32,2,128,128]{3,2,1,0:T(8,128)(2,1)} %broadcast_select_fusion.1), calls=%async_computation.1 | async-start | bytes 4194304 | tf_op jit(solution)/shard_map/all_to_all | solution.py:108
  46.3 101.3 %copy-start.11 = (bf16[2048,128]{1,0:T(8,128)(2,1)S(1)}, bf16[2048,128]{1,0:T(8,128)(2,1)}, u32[]{:S(2)}) copy-start(bf16[2048,128]{1,0:T(8,128)(2,1)} %param.13) | copy-start | bytes 1572868
  147.5 3.0 copy-start.4
  176.7 5.7 %copy-start.12 = (bf16[2048,128]{1,0:T(8,128)(2,1)S(1)}, bf16[2048,128]{1,0:T(8,128)(2,1)}, u32[]{:S(2)}) copy-start(bf16[2048,128]{1,0:T(8,128)(2,1)} %param.20) | copy-start | bytes 1572868
  178.2 14.6 %all-to-all-start.3 = ((bf16[16,48,512]{2,1,0:T(8,128)(2,1)}), bf16[16,48,512]{2,1,0:T(8,128)(2,1)S(1)}, u32[]{:S(2)}, u32[]{:S(2)}) async-start(bf16[16,48,512]{2,1,0:T(8,128)(2,1)} %broadcast_in_dim.44), calls=%async_computation.3 | async-start | bytes 1572864 | tf_op jit(solution)/shard_map/all_to_all | solution.py:42
  185.3 0.7 copy-start.8
  192.8 2.5 copy-start.2
  202.0 11.0 %copy-start.13 = (s32[8]{0:T(128)S(1)}, s32[8]{0:T(128)}, u32[]{:S(2)}) copy-start(s32[8]{0:T(128)} %param.18) | copy-start | bytes 100
  202.0 11.0 %copy-start.10 = (f32[128]{0:T(128)S(1)}, f32[128]{0:T(128)}, u32[]{:S(2)}) copy-start(f32[128]{0:T(128)} %param.19) | copy-start | bytes 1540
  202.0 109.6 %copy-start.7 = (f32[1024,128]{1,0:T(8,128)S(1)}, f32[1024,128]{1,0:T(8,128)}, u32[]{:S(2)}) copy-start(f32[1024,128]{1,0:T(8,128)} %param.15) | copy-start | bytes 1572868
  202.0 109.5 %all-to-all-start.6 = ((bf16[32,2,128,128]{3,2,1,0:T(8,128)(2,1)}), bf16[32,2,128,128]{3,2,1,0:T(8,128)(2,1)S(1)}, u32[]{:S(2)}, u32[]{:S(2)}) async-start(bf16[32,2,128,128]{3,2,1,0:T(8,128)(2,1)} %bitcast.22), calls=%async_computation.6 | async-start | bytes 4194304 | tf_op jit(solution)/shard_map/all_to_all | solution.py:137
  422.1 2.0 copy-start.3
  424.1 1.9 copy-start.9
  429.5 4.6 copy-start.6
  429.5 5.5 %copy-start.5 = (f32[8,128,128]{2,0,1:T(8,128)S(1)}, f32[8,128,128]{2,0,1:T(8,128)}, u32[]{:S(2)}) copy-start(f32[8,128,128]{2,0,1:T(8,128)} %get-tuple-element.7) | copy-start | bytes 1572868
  429.5 46.0 %all-to-all-start.5 = ((bf16[16,768,128]{2,1,0:T(8,128)(2,1)}), bf16[16,768,128]{2,1,0:T(8,128)(2,1)}, u32[]{:S(2)}, u32[]{:S(2)}) async-start(bf16[16,768,128]{2,1,0:T(8,128)(2,1)} %bitcast.82), calls=%async_computation.5 | async-start | bytes 6291456 | tf_op jit(solution)/shard_map/all_to_all | solution.py:53
Sparse Core Ops, SparseCore 0:
  11.6 87.5 all-gather.1
where the time goes:
time: 491 us; the launch traced here: 485 us
  waiting for transfers between devices  240 us (49%)
  blocking collectives  159 us (32%)
  starting transfers between devices  24.3 us (5%)
  local copies, waits for them, and re-layouts  22.4 us (5%)
  matrix products  16.6 us (3%)
  between operations  14.3 us (3%)
  other arithmetic  8.47 us (2%)
    all_to_all x1, blocking collectives, per_device(): lax.all_to_all(reply_values, 'tok', split_axis=0, concat_axis=0, tiled=True)  106 us
    all_to_all x1, waiting for transfers between devices, per_device(): lax.all_to_all(reply_keys, 'tok', split_axis=0, concat_axis=0, tiled=True)  99.2 us
    all_to_all x1, waiting for transfers between devices, per_device(): lax.all_to_all(outgoing.reshape(owners, capacity, page_slots, col_width),...  97.1 us
    all_to_all x1, waiting for transfers between devices, summed_on_arrival(): lax.all_to_all(pieces, axis, split_axis=0, concat_axis=0, tiled=True)  39.6 us
    all_to_all x1, blocking collectives, per_device(): lax.all_to_all(wanted, 'tok', split_axis=0, concat_axis=0, tiled=True)  28.3 us
    all_to_all x1, blocking collectives, sum_at_owner(): pieces = lax.all_to_all(split_up(shard, dim, count), axis, 0, 0, tiled=True)  25.5 us
    all_to_all x1, starting transfers between devices, per_device(): lax.all_to_all(outgoing.reshape(owners, capacity, page_slots, col_width),...  10.9 us
  transfers between devices with their start and end apart: 5, of which 4 were waited for; matrix products, arithmetic and copies ran while one was open for 3% of the time, Pallas kernels for 0%

commit v1 on v0

v1 whole, which is shorter than its diff:
```python
import jax
import jax.numpy as jnp
from jax import lax
from jax.experimental import pallas as pl
from jax.experimental.pallas import tpu as pltpu
from jax.sharding import PartitionSpec as P

KW = 2048
STEP = 64
MOMENTUM_RATE = 0.9
LEARN_RATE = 1.0

NZ = 16
NX = 4
NCOL = 16
ROWS = 768
NB = 12
PICKS = 4
BLK = 64
PAGE = 128
LANE = 128
OWN = 1024
SHARE = ROWS // NCOL
LIST = PICKS * PAGE
HALF = ROWS // 2
CNT = 16
GROWS = OWN + CNT
MESH = pl.DeviceIdType.MESH
HOPS = ((8, 7), (7, 8))
ANY = pl.BlockSpec(memory_space=pl.ANY)
VM = pl.BlockSpec(memory_space=pltpu.VMEM)
SM = pl.BlockSpec(memory_space=pltpu.SMEM)


class Place:
    def __init__(self):
        self.tok = lax.axis_index("tok")
        self.col = lax.axis_index("col")
        self.z = self.tok // 2
        self.c = self.tok % 2
        self.x = self.col // NX
        self.y = self.col % NX
        self.sib = (self.zc(0, 1 - self.c), self.col)
        self.zn = ((self.zc(1, self.c), self.col), (self.zc(-1, self.c), self.col))

    def zc(self, dz, c):
        return ((self.z + dz + NZ) % NZ) * 2 + c

    def xy(self, dx, dy):
        return ((self.x + dx + NX) % NX) * NX + (self.y + dy + NX) % NX

    def peer(self, dx, dy):
        return (self.tok, self.xy(dx, dy))


def remote(src, dst, ssem, rsem, dev):
    return pltpu.make_async_remote_copy(
        src_ref=src, dst_ref=dst, send_sem=ssem, recv_sem=rsem, device_id=dev, device_id_type=MESH
    )


def greet(devices):
    barrier = pltpu.get_barrier_semaphore()
    for dev in devices:
        pl.semaphore_signal(barrier, inc=1, device_id=dev, device_id_type=MESH)
    pl.semaphore_wait(barrier, len(devices))


def z_gather(at, src, dst, rsend, rrecv, ssend, srecv, own):
    half = OWN // 2
    sent = []

    def start(copy):
        copy.start()
        sent.append(copy)

    for d in range(2):
        for h in range(2):
            rows = pl.ds(h * half, half)
            start(remote(src.at[rows], dst.at[at.tok, rows], rsend.at[d, h, 0], rrecv.at[d, h, 0], at.zn[d]))
    start(remote(src, dst.at[at.tok], own.at[0], own.at[1], at.sib))
    local = pltpu.make_async_copy(src, dst.at[at.tok], own.at[2])
    local.start()
    yield
    for s in range(1, 9):
        for d in range(2):
            for h in range(2):
                if s > HOPS[d][h]:
                    continue
                rows = pl.ds(h * half, half)
                block = dst.at[at.zc(-s if d == 0 else s, at.c), rows]
                remote(block, block, rsend.at[d, h, s - 1], rrecv.at[d, h, s - 1], at.zn[d]).wait_recv()
                if s < HOPS[d][h]:
                    start(remote(block, block, rsend.at[d, h, s], rrecv.at[d, h, s], at.zn[d]))
                start(remote(block, block, ssend.at[d, h, s - 1], srecv.at[d, h, s - 1], at.sib))
        yield
    mine = dst.at[at.zc(0, 1 - at.c)]
    remote(mine, mine, own.at[0], own.at[1], at.sib).wait_recv()
    for d in range(2):
        for h in range(2):
            for s in range(1, HOPS[d][h] + 1):
                rows = pl.ds(h * half, half)
                block = dst.at[at.zc(-s if d == 0 else s, 1 - at.c), rows]
                remote(block, block, ssend.at[d, h, s - 1], srecv.at[d, h, s - 1], at.sib).wait_recv()
    for copy in sent:
        copy.wait_send()
    local.wait()
    yield


def xy_gather(at, src, dst, sends, recvs, local_sem, first):
    sent = []
    lo, hi = pl.ds(0, HALF), pl.ds(HALF, HALF)

    def shift(a, b):
        return (a, b) if first == 0 else (b, a)

    def dev(a, b):
        return at.peer(*shift(a, b))

    def slot(a, b):
        return dst.at[at.xy(*shift(a, b))]

    def start(block, k, to):
        copy = remote(block, block, sends.at[k], recvs.at[k], to)
        copy.start()
        sent.append(copy)

    def wait(block, k, to):
        remote(block, block, sends.at[k], recvs.at[k], to).wait_recv()

    for k, a in ((0, 1), (1, -1)):
        copy = remote(src, slot(0, 0), sends.at[k], recvs.at[k], dev(a, 0))
        copy.start()
        sent.append(copy)
    for k, b in ((4, 1), (5, -1)):
        copy = remote(src, slot(0, 0), sends.at[k], recvs.at[k], dev(0, b))
        copy.start()
        sent.append(copy)
    local = pltpu.make_async_copy(src, slot(0, 0), local_sem)
    local.start()
    yield
    wait(slot(-1, 0), 0, dev(1, 0))
    start(slot(-1, 0).at[lo], 2, dev(1, 0))
    wait(slot(1, 0), 1, dev(-1, 0))
    start(slot(1, 0).at[hi], 3, dev(-1, 0))
    for item, a in ((1, -1), (2, 1)):
        start(slot(a, 0), 4 + 4 * item, dev(0, 1))
        start(slot(a, 0), 5 + 4 * item, dev(0, -1))
    yield
    wait(slot(2, 0).at[lo], 2, dev(1, 0))
    wait(slot(2, 0).at[hi], 3, dev(-1, 0))
    start(slot(2, 0), 4 + 4 * 3, dev(0, 1))
    start(slot(2, 0), 5 + 4 * 3, dev(0, -1))
    yield
    for item, a in ((0, 0), (1, -1), (2, 1), (3, 2)):
        k = 4 + 4 * item
        wait(slot(a, -1), k, dev(0, 1))
        start(slot(a, -1).at[lo], k + 2, dev(0, 1))
        wait(slot(a, 1), k + 1, dev(0, -1))
        start(slot(a, 1).at[hi], k + 3, dev(0, -1))
        yield
    for item, a in ((0, 0), (1, -1), (2, 1), (3, 2)):
        k = 4 + 4 * item
        wait(slot(a, 2).at[lo], k + 2, dev(0, 1))
        wait(slot(a, 2).at[hi], k + 3, dev(0, -1))
    for copy in sent:
        copy.wait_send()
    local.wait()
    yield


def together(*parts):
    parts = list(parts)
    while parts:
        alive = []
        for part in parts:
            try:
                next(part)
                alive.append(part)
            except StopIteration:
                pass
        parts = alive


def dma(*shape):
    return pltpu.SemaphoreType.DMA(shape)


Z_SEMS = [dma(2, 2, 8), dma(2, 2, 8), dma(2, 2, 8), dma(2, 2, 8), dma(3)]


def params(ident, vmem=56 << 20):
    return pltpu.CompilerParams(collective_id=ident, has_side_effects=True, vmem_limit_bytes=vmem)


def gather_kernel(keys, tokens, cotangent, kall, tall, call, *sems):
    at = Place()
    greet([at.zn[0], at.zn[1], at.sib, at.peer(1, 0), at.peer(-1, 0), at.peer(0, 1), at.peer(0, -1)])
    together(
        z_gather(at, keys, kall, *sems[:5]),
        xy_gather(at, tokens, tall, sems[5], sems[6], sems[9].at[0], 0),
        xy_gather(at, cotangent, call, sems[7], sems[8], sems[9].at[1], 1),
    )


def gather(keys, tokens, cotangent):
    blocks = jax.ShapeDtypeStruct((NCOL, ROWS, LANE), jnp.bfloat16)
    return pl.pallas_call(
        gather_kernel,
        out_shape=(jax.ShapeDtypeStruct((2 * NZ, OWN, LANE), jnp.bfloat16), blocks, blocks),
        in_specs=[ANY] * 3,
        out_specs=(ANY,) * 3,
        scratch_shapes=Z_SEMS + [dma(20), dma(20), dma(20), dma(20), dma(2)],
        compiler_params=params(0),
    )(keys, tokens, cotangent)


def fetch_pages(pids, pages, buf, sem):
    copies = []
    for n in range(NB * PICKS):
        copy = pltpu.make_async_copy(pages.at[pids[n // PICKS, n % PICKS]], buf.at[n], sem.at[n])
        copy.start()
        copies.append(copy)
    return copies


def project_kernel(pids, tall, call, wq, wg, wo, pages, scores, act, grads, qbuf, kbuf, sem):
    copies = fetch_pages(pids, pages, kbuf, sem)
    tile = 128

    def step(r, carry):
        rows = pl.ds(pl.multiple_of(r * tile, tile), tile)
        qs = jnp.zeros((tile, LANE), jnp.float32)
        gs = jnp.zeros((tile, LANE), jnp.float32)
        cs = jnp.zeros((tile, LANE), jnp.float32)
        for k in range(NCOL):
            t = tall[k, rows, :]
            qs += jnp.dot(t, wq[k], preferred_element_type=jnp.float32)
            gs += jnp.dot(t, wg[k], preferred_element_type=jnp.float32)
            cs += lax.dot_general(
                call[k, rows, :],
                wo[:, k * LANE : (k + 1) * LANE],
                (((1,), (1,)), ((), ())),
                preferred_element_type=jnp.float32,
            )
        a = gs / (1.0 + jnp.exp(-gs))
        act[rows, :] = a
        grads[rows, :] = (cs * a).astype(jnp.bfloat16)
        qbuf[rows, :] = qs.astype(jnp.bfloat16)
        return carry

    lax.fori_loop(0, ROWS // tile, step, 0)
    for copy in copies:
        copy.wait()

    def block(b, carry):
        rows = pl.ds(pl.multiple_of(b * BLK, BLK), BLK)
        q = qbuf[rows, :]
        for i in range(PICKS):
            scores[rows, i * PAGE : (i + 1) * PAGE] = lax.dot_general(
                q, kbuf[b * PICKS + i], (((1,), (1,)), ((), ())), preferred_element_type=jnp.float32
            )
        return carry

    lax.fori_loop(0, NB, block, 0)


def project(pids, tall, call, wq, wg, wo, pages):
    return pl.pallas_call(
        project_kernel,
        out_shape=(
            jax.ShapeDtypeStruct((ROWS, LIST), jnp.float32),
            jax.ShapeDtypeStruct((ROWS, LANE), jnp.float32),
            jax.ShapeDtypeStruct((ROWS, LANE), jnp.bfloat16),
        ),
        in_specs=[SM] + [VM] * 5 + [ANY],
        out_specs=(VM,) * 3,
        scratch_shapes=[
            pltpu.VMEM((ROWS, LANE), jnp.bfloat16),
            pltpu.VMEM((NB * PICKS, PAGE, LANE), jnp.bfloat16),
            dma(NB * PICKS),
        ],
        compiler_params=pltpu.CompilerParams(vmem_limit_bytes=56 << 20),
    )(pids, tall, call, wq, wg, wo, pages)


def peers(at):
    return [(dx, dy) for dx in (0, 1, -1, 2) for dy in (0, 1, -1, 2) if (dx, dy) != (0, 0)]


def weigh(at, scores, weights, got, share, wsend, wrecv, ssend, srecv):
    around = peers(at)
    sent = []
    for k, (dx, dy) in enumerate(around):
        to = at.xy(dx, dy)
        copy = remote(scores.at[to], got.at[k], ssend.at[k], srecv.at[k], at.peer(dx, dy))
        copy.start()
        sent.append(copy)
    for _ in range(5):
        yield
    for k, (dx, dy) in enumerate(around):
        remote(got.at[k], got.at[k], ssend.at[k], srecv.at[k], at.peer(dx, dy)).wait_recv()
    total = scores[at.col]
    for k in range(len(around)):
        total = total + got[k]
    total = total * (KW**-0.5)
    e = jnp.exp(total - jnp.max(total, axis=1, keepdims=True))
    w = (e / jnp.sum(e, axis=1, keepdims=True)).astype(jnp.bfloat16)
    share[...] = w
    weights[at.col] = w
    for k, (dx, dy) in enumerate(around):
        copy = remote(share, weights.at[at.col], wsend.at[k], wrecv.at[k], at.peer(dx, dy))
        copy.start()
        sent.append(copy)
    yield
    yield
    yield
    for k, (dx, dy) in enumerate(around):
        block = weights.at[at.xy(-dx, -dy)]
        remote(block, block, wsend.at[k], wrecv.at[k], at.peer(dx, dy)).wait_recv()
    for copy in sent:
        copy.wait_send()
    yield


def weigh_kernel(stored, scores, vall, wout, got, share, weights, *sems):
    at = Place()
    greet([at.zn[0], at.zn[1], at.sib] + [at.peer(dx, dy) for dx, dy in peers(at)])
    together(
        z_gather(at, stored, vall, *sems[:5]),
        weigh(at, scores, weights, got, share, *sems[5:]),
    )
    wout[...] = weights[...]


def weigh_call(stored, scores):
    return pl.pallas_call(
        weigh_kernel,
        out_shape=(
            jax.ShapeDtypeStruct((2 * NZ, OWN, LANE), jnp.bfloat16),
            jax.ShapeDtypeStruct((NCOL, SHARE, LIST), jnp.bfloat16),
        ),
        in_specs=[ANY, VM],
        out_specs=(ANY, VM),
        scratch_shapes=[
            pltpu.VMEM((NCOL - 1, SHARE, LIST), jnp.float32),
            pltpu.VMEM((SHARE, LIST), jnp.bfloat16),
            pltpu.VMEM((NCOL, SHARE, LIST), jnp.bfloat16),
        ]
        + Z_SEMS
        + [dma(15)] * 4,
        compiler_params=params(1),
    )(stored, scores)


def mix_kernel(pids, weights, act, grads, wo, pages, outa, outb, acc, gated, vbuf, sem):
    copies = fetch_pages(pids, pages, vbuf, sem)

    def clear(n, carry):
        acc[n] = jnp.zeros((GROWS, LANE), jnp.bfloat16)
        return carry

    lax.fori_loop(0, 2 * NZ, clear, 0)
    row = lax.broadcasted_iota(jnp.int32, (2 * NZ, CNT, LANE), 1)
    page = lax.broadcasted_iota(jnp.int32, (2 * NZ, CNT, LANE), 0) * 8 + row
    page = jnp.where(row < 8, page, -1)
    count = jnp.zeros((2 * NZ, CNT, LANE), jnp.float32)
    for n in range(NB * PICKS):
        count += jnp.where(page == pids[n // PICKS, n % PICKS], 1.0, 0.0)
    acc[:, OWN:, :] = count.astype(jnp.bfloat16)

    def grad(b, carry):
        rows = pl.ds(pl.multiple_of(b * BLK, BLK), BLK)
        g = grads[rows, :]
        for i in range(PICKS):
            w = weights[rows, i * PAGE : (i + 1) * PAGE]
            s = lax.dot_general(w, g, (((0,), (0,)), ((), ())), preferred_element_type=jnp.float32)
            p = pids[b, i]
            at = (p // 8, pl.ds(pl.multiple_of((p % 8) * PAGE, PAGE), PAGE))
            acc[at] = (acc[at].astype(jnp.float32) + s).astype(jnp.bfloat16)
        return carry

    lax.fori_loop(0, NB, grad, 0)
    for copy in copies:
        copy.wait()

    def block(b, carry):
        rows = pl.ds(pl.multiple_of(b * BLK, BLK), BLK)
        m = jnp.zeros((BLK, LANE), jnp.float32)
        for i in range(PICKS):
            m += jnp.dot(
                weights[rows, i * PAGE : (i + 1) * PAGE],
                vbuf[b * PICKS + i],
                preferred_element_type=jnp.float32,
            )
        gated[rows, :] = (m * act[rows, :]).astype(jnp.bfloat16)
        return carry

    lax.fori_loop(0, NB, block, 0)
    for k in range(NCOL):
        o = jnp.dot(
            gated[...], wo[:, k * LANE : (k + 1) * LANE], preferred_element_type=jnp.float32
        ).astype(jnp.bfloat16)
        outa[k] = o[:HALF]
        outb[(k % NX) * NX + k // NX] = o[HALF:]


def mix(pids, weights, act, grads, wo, pages):
    halves = jax.ShapeDtypeStruct((NCOL, HALF, LANE), jnp.bfloat16)
    return pl.pallas_call(
        mix_kernel,
        out_shape=(halves, halves, jax.ShapeDtypeStruct((2 * NZ, GROWS, LANE), jnp.bfloat16)),
        in_specs=[SM] + [VM] * 4 + [ANY],
        out_specs=(VM,) * 3,
        scratch_shapes=[
            pltpu.VMEM((ROWS, LANE), jnp.bfloat16),
            pltpu.VMEM((NB * PICKS, PAGE, LANE), jnp.bfloat16),
            dma(NB * PICKS),
        ],
        compiler_params=pltpu.CompilerParams(vmem_limit_bytes=56 << 20),
    )(pids, weights, act, grads, wo, pages)


def sub(h):
    return (0, 528, 176) if h == 0 else (528, 512, 128)


def z_reduce(at, mine, total, theirs, stage, land, xsend, xrecv, rsend, rrecv):
    sent = []
    for n, off in enumerate((8, 7, -7, 6, -6, 5, -5, 4, -4, 3, -3, 2, -2, 1, -1, 0)):
        copy = remote(
            mine.at[at.zc(off, 1 - at.c)], theirs.at[off + 7], xsend.at[off + 7], xrecv.at[off + 7], at.sib
        )
        copy.start()
        sent.append(copy)

    def wait_sib(off):
        block = theirs.at[off + 7]
        remote(block, block, xsend.at[off + 7], xrecv.at[off + 7], at.sib).wait_recv()

    def landed(d, h, s):
        first, size, tile = sub(h)
        block = land.at[d, s, pl.ds(first, size)]
        remote(block, block, rsend.at[d, h, s], rrecv.at[d, h, s], at.zn[d]).wait_recv()

    wait_sib(8)
    for s in range(8):
        if s < 7:
            wait_sib(7 - s)
            wait_sib(s - 7)
        for d in range(2):
            for h in range(2):
                if s >= HOPS[d][h]:
                    continue
                far = HOPS[d][h] - s
                off = far if d == 0 else -far
                buf = 8 if far == 8 else off
                owner = at.zc(off, at.c)
                first, size, tile = sub(h)
                if s:
                    landed(d, h, s - 1)
                for t in range(size // tile):
                    rows = pl.ds(first + t * tile, tile)
                    v = mine[owner, rows, :].astype(jnp.float32) + theirs[buf + 7, rows, :].astype(jnp.float32)
                    if s:
                        v = v + land[d, s - 1, rows, :].astype(jnp.float32)
                    stage[d, s, rows, :] = v.astype(jnp.bfloat16)
                rows = pl.ds(first, size)
                copy = remote(
                    stage.at[d, s, rows], land.at[d, s, rows], rsend.at[d, h, s], rrecv.at[d, h, s], at.zn[d]
                )
                copy.start()
                sent.append(copy)
        yield
    wait_sib(0)
    for h in range(2):
        first, size, tile = sub(h)
        for d in range(2):
            landed(d, h, HOPS[d][h] - 1)
        for t in range(size // tile):
            rows = pl.ds(first + t * tile, tile)
            v = mine[at.tok, rows, :].astype(jnp.float32) + theirs[7, rows, :].astype(jnp.float32)
            for d in range(2):
                v = v + land[d, HOPS[d][h] - 1, rows, :].astype(jnp.float32)
            total[rows, :] = v
    for copy in sent:
        copy.wait_send()
    yield


def xy_reduce(at, terms, out, first, got1, part, got2, send1, recv1, send2, recv2):
    sent = []
    mine = (at.x, at.y) if first == 0 else (at.y, at.x)

    def dev(a, b):
        return at.peer(a, b) if first == 0 else at.peer(b, a)

    for k, a in enumerate((2, 1, -1)):
        line = (mine[0] + a + NX) % NX
        copy = remote(terms.at[pl.ds(line * NX, NX)], got1.at[k], send1.at[k], recv1.at[k], dev(a, 0))
        copy.start()
        sent.append(copy)
    for _ in range(4):
        yield
    for k, a in enumerate((2, 1, -1)):
        remote(got1.at[k], got1.at[k], send1.at[k], recv1.at[k], dev(a, 0)).wait_recv()
    for b in range(NX):
        v = terms[mine[0] * NX + b].astype(jnp.float32)
        for k in range(3):
            v = v + got1[k, b].astype(jnp.float32)
        part[b] = v.astype(jnp.bfloat16)
    for k, b in enumerate((2, 1, -1)):
        copy = remote(part.at[(mine[1] + b + NX) % NX], got2.at[k], send2.at[k], recv2.at[k], dev(0, b))
        copy.start()
        sent.append(copy)
    yield
    yield
    for k, b in enumerate((2, 1, -1)):
        remote(got2.at[k], got2.at[k], send2.at[k], recv2.at[k], dev(0, b)).wait_recv()
    v = part[mine[1]].astype(jnp.float32)
    for k in range(3):
        v = v + got2[k].astype(jnp.float32)
    out[pl.ds(first * HALF, HALF), :] = v.astype(jnp.bfloat16)
    for copy in sent:
        copy.wait_send()
    yield


def reduce_kernel(outa, outb, acc, out, total, *rest):
    at = Place()
    greet(
        [at.zn[0], at.zn[1], at.sib]
        + [at.peer(a, 0) for a in (1, -1, 2)]
        + [at.peer(0, a) for a in (1, -1, 2)]
    )
    together(
        xy_reduce(at, outa, out, 0, *rest[:7]),
        xy_reduce(at, outb, out, 1, *rest[7:14]),
        z_reduce(at, acc, total, *rest[14:]),
    )


def reduce_call(outa, outb, acc):
    xy = [
        pltpu.VMEM((3, NX, HALF, LANE), jnp.bfloat16),
        pltpu.VMEM((NX, HALF, LANE), jnp.bfloat16),
        pltpu.VMEM((3, HALF, LANE), jnp.bfloat16),
    ] + [dma(3)] * 4
    return pl.pallas_call(
        reduce_kernel,
        out_shape=(
            jax.ShapeDtypeStruct((ROWS, LANE), jnp.bfloat16),
            jax.ShapeDtypeStruct((GROWS, LANE), jnp.float32),
        ),
        in_specs=[VM] * 3,
        out_specs=(VM,) * 2,
        scratch_shapes=xy
        + xy
        + [
            pltpu.VMEM((NZ, GROWS, LANE), jnp.bfloat16),
            pltpu.VMEM((2, 8, GROWS, LANE), jnp.bfloat16),
            pltpu.VMEM((2, 8, GROWS, LANE), jnp.bfloat16),
            dma(16),
            dma(16),
            dma(2, 2, 8),
            dma(2, 2, 8),
        ],
        compiler_params=params(2),
    )(outa, outb, acc)


def per_device(
    tokens,
    cotangent,
    query_weight,
    slot_keys,
    values,
    momentum,
    page_ids,
    last_step,
    decay_rate,
    gate_weight,
    out_weight,
):
    pages_local = last_step.shape[0]
    elapsed = (STEP - last_step).astype(jnp.float32)
    factor = jnp.exp(-elapsed[:, None] * decay_rate[None, :])[:, None, :]
    stored = values.reshape(pages_local, PAGE, LANE)
    decayed = (stored * factor).astype(jnp.bfloat16).reshape(OWN, LANE)
    kall, tall, call = gather(slot_keys, tokens, cotangent)
    scores, act, grads = project(
        page_ids,
        tall,
        call,
        query_weight.reshape(NCOL, LANE, LANE),
        gate_weight.reshape(NCOL, LANE, LANE),
        out_weight,
        kall.reshape(-1, PAGE, LANE),
    )
    vall, weights = weigh_call(decayed, scores.reshape(NCOL, SHARE, LIST))
    outa, outb, acc = mix(
        page_ids, weights.reshape(ROWS, LIST), act, grads, out_weight, vall.reshape(-1, PAGE, LANE)
    )
    layer_out, total = reduce_call(outa, outb, acc)
    page_grad = total[:OWN].reshape(pages_local, PAGE, LANE)
    touched = (total[OWN : OWN + pages_local, 0] > 0.5)[:, None, None]
    moment = momentum.reshape(pages_local, PAGE, LANE)
    new_momentum = jnp.where(touched, MOMENTUM_RATE * moment + page_grad * factor, moment)
    new_values = jnp.where(touched, stored * factor - LEARN_RATE * new_momentum, stored)
    return (layer_out, new_values.reshape(OWN, LANE), new_momentum.reshape(OWN, LANE))


def solution(mesh):
    in_specs = (
        P("tok", "col"),
        P("tok", "col"),
        P(None, "col"),
        P("tok", "col"),
        P("tok", "col"),
        P("tok", "col"),
        P("tok", None),
        P("tok"),
        P("col"),
        P(None, "col"),
        P("col", None),
    )
    out_specs = (P("tok", "col"), P("tok", "col"), P("tok", "col"))
    return jax.shard_map(
        per_device, mesh=mesh, in_specs=in_specs, out_specs=out_specs, check_vma=False
    )
```

time: 491 us -> 224 us (0.46)
  waiting for transfers between devices: 240 us -> 0 us
  Pallas kernels: 0 us -> 212 us
  blocking collectives: 159 us -> 0 us
  starting transfers between devices: 24.3 us -> 0 us
  local copies, waits for them, and re-layouts: 22.4 us -> 3.07 us
  matrix products: 16.6 us -> 0 us
  between operations: 14.3 us -> 0.69 us
    all_to_all x4 -> x0, waiting for transfers between devices: 240 us -> none  [the longest x1 99.2 us: per_device(): lax.all_to_all(reply_keys, 'tok', split_axis=0, concat_axis=0, tiled=True)]
    pallas_call x0 -> x5, Pallas kernels: none -> 212 us  [the longest x1 70.5 us: gather(): pl.pallas_call(gather_kernel, out_shape=(jax.ShapeDtypeStruct((2 * NZ, OW...]
    all_to_all x3 -> x0, blocking collectives: 159 us -> none  [the longest x1 106 us: per_device(): lax.all_to_all(reply_values, 'tok', split_axis=0, concat_axis=0, tiled=True)]
    all_to_all x4 -> x0, starting transfers between devices: 24.3 us -> none  [the longest x1 10.9 us: per_device(): lax.all_to_all(outgoing.reshape(owners, capacity, page_slots, col_width),...]
    dot_general x8 -> x0, matrix products: 16.6 us -> none  [the longest x1 3.74 us: per_device(): jnp.dot(page_match.astype(jnp.bfloat16), returned.reshape(send_slots, pag...]
    scatter x1 -> x0, local copies, waits for them, and re-layouts: 6.62 us -> none  [per_device(): outgoing.at[send_slot]]
    gather x4 -> x0, local copies, waits for them, and re-layouts: 5.81 us -> none  [the longest x1 1.96 us: per_device(): got_values.reshape(send_slots, page_slots, col_width)[send_slot]]
  transfers between devices with their start and end apart: 5 -> 0, of which waited for: 4 -> 0; matrix products, arithmetic and copies ran while one was open for 3% -> 0% of each run, Pallas kernels for 0% -> 0%
where the time goes in v1:
time: 224 us; the launch traced here: 222 us
  Pallas kernels  212 us (95%)
  other arithmetic  6.17 us (3%)
  local copies, waits for them, and re-layouts  3.07 us (1%)
    pallas_call x1, Pallas kernels, gather(): pl.pallas_call(gather_kernel, out_shape=(jax.ShapeDtypeStruct((2 * NZ, OW...  70.5 us
    pallas_call x1, Pallas kernels, weigh_call(): pl.pallas_call(weigh_kernel, out_shape=(jax.ShapeDtypeStruct((2 * NZ, OWN...  59 us
    pallas_call x1, Pallas kernels, reduce_call(): pl.pallas_call(reduce_kernel, out_shape=(jax.ShapeDtypeStruct((ROWS, LANE...  56.5 us
    pallas_call x1, Pallas kernels, mix(): pl.pallas_call(mix_kernel, out_shape=(halves, halves, jax.ShapeDtypeStruc...  13.9 us
    pallas_call x1, Pallas kernels, project(): pl.pallas_call(project_kernel, out_shape=(jax.ShapeDtypeStruct((ROWS, LIS...  11.8 us

profile of v1, /device:TPU:1, one launch (start us, length us, event | category | flops | bytes accessed | tf_op | source)
XLA Modules:
  0.0 221.6 jit_solution(3163008197640799019)
XLA Ops:
  0.6 0.7 convert_negate_fusion
  1.3 0.7 multiply_exponential_fusion
  2.0 1.4 copy.17.pids
  3.4 1.8 fusion.2.stored
  5.2 70.5 %shard_map.130 = (bf16[32,1024,128]{2,1,0:T(8,128)(2,1)}, bf16[16,768,128]{2,1,0:T(8,128)(2,1)}, bf16[16,768,128]{2,1,0:T(8,128)(2,1)}) custom-call(bf16[1024,128]{1,0:T(8,128)(2,1)} %keys.1, bf16[768,128]{1,0:T(8,128)(2,1)} %tokens.1, bf16[768,128]{1,0:T(8,128)(2,1)} %cotangent.1), custom_call_target="tpu_custom_call" | custom-call | tf_op jit(solution)/shard_map/pallas_call | solution.py:209
  75.6 11.8 %shard_map.131 = (f32[768,512]{1,0:T(8,128)}, f32[768,128]{1,0:T(8,128)}, bf16[768,128]{1,0:T(8,128)(2,1)}) custom-call(s32[12,4]{1,0:T(8,128)} %copy.17.pids, bf16[16,768,128]{2,1,0:T(8,128)(2,1)} %get-tuple-element.16.tall, bf16[16,768,128]{2,1,0:T(8,128)(2,1)} %get-tuple-element.17.call, bf16[16,128,128]{2,1,0:T(8,128)(2,1)} %bitcast.24, ...), custom_call_target="tpu_custom_call" | custom-call | tf_op jit(solution)/shard_map/pallas_call | solution.py:270
  87.4 59.0 %shard_map.132 = (bf16[32,1024,128]{2,1,0:T(8,128)(2,1)}, bf16[16,48,512]{2,1,0:T(8,128)(2,1)}) custom-call(bf16[1024,128]{1,0:T(8,128)(2,1)} %fusion.2.stored, f32[16,48,512]{2,1,0:T(8,128)} %bitcast.22), custom_call_target="tpu_custom_call" | custom-call | tf_op jit(solution)/shard_map/pallas_call | solution.py:338
  146.4 13.9 %shard_map.133 = (bf16[16,384,128]{2,1,0:T(8,128)(2,1)}, bf16[16,384,128]{2,1,0:T(8,128)(2,1)}, bf16[32,1040,128]{2,1,0:T(8,128)(2,1)}) custom-call(s32[12,4]{1,0:T(8,128)} %copy.17.pids, bf16[768,512]{1,0:T(8,128)(2,1)} %bitcast.23, f32[768,128]{1,0:T(8,128)} %get-tuple-element.21.act, bf16[768,128]{1,0:T(8,128)(2,1)} %get-tuple-element.22.grads, ...), custom_call_target="tpu_custom_call" | custom-call | tf_op jit(solution)/shard_map/pallas_call | solution.py:411
  160.3 0.0 copy-start
  160.3 0.0 copy-start.1
  160.4 56.5 %shard_map.134 = (bf16[768,128]{1,0:T(8,128)(2,1)}, f32[1040,128]{1,0:T(8,128)}) custom-call(bf16[16,384,128]{2,1,0:T(8,128)(2,1)} %get-tuple-element.24.outa, bf16[16,384,128]{2,1,0:T(8,128)(2,1)} %get-tuple-element.25.outb, bf16[32,1040,128]{2,1,0:T(8,128)(2,1)} %get-tuple-element.26.acc), custom_call_target="tpu_custom_call" | custom-call | tf_op jit(solution)/shard_map/pallas_call | solution.py:550
  216.9 0.8 fusion.3
  217.7 0.1 broadcast_bitcast_fusion
  217.8 0.0 copy-done
  217.8 0.0 copy-done.1
  217.8 2.2 subtract_select_fusion
  220.0 1.6 copy.19
Async XLA Ops:
  160.3 57.4 %copy-start = (f32[1024,128]{1,0:T(8,128)S(1)}, f32[1024,128]{1,0:T(8,128)}, u32[]{:S(2)}) copy-start(f32[1024,128]{1,0:T(8,128)} %param.15) | copy-start | bytes 1572868
  160.3 57.4 %copy-start.1 = (f32[1024,128]{1,0:T(8,128)S(1)}, f32[1024,128]{1,0:T(8,128)}, u32[]{:S(2)}) copy-start(f32[1024,128]{1,0:T(8,128)} %param.16) | copy-start | bytes 1572868

commit v2 on v0

v2 whole, which is shorter than its diff:
```python
import jax
import jax.numpy as jnp
from jax import lax
from jax.experimental import pallas as pl
from jax.experimental.pallas import tpu as pltpu
from jax.sharding import PartitionSpec as P

KW = 2048
STEP = 64
MOMENTUM_RATE = 0.9
LEARN_RATE = 1.0

NZ = 16
NX = 4
NCOL = 16
ROWS = 768
NB = 12
PICKS = 4
PAIRS = NB * PICKS
BLK = 64
PAGE = 128
LANE = 128
LOCAL = 8
OWNERS = 2 * NZ
PAGES = OWNERS * LOCAL
OWN = 1024
SHARE = ROWS // NCOL
HALF = ROWS // 2
CNT = 16
GROWS = OWN + CNT
MESH = pl.DeviceIdType.MESH
HOPS = ((8, 7), (7, 8))
VM = pl.BlockSpec(memory_space=pltpu.VMEM)
SM = pl.BlockSpec(memory_space=pltpu.SMEM)
F32 = jnp.float32
BF16 = jnp.bfloat16


class Place:
    def __init__(self):
        self.tok = lax.axis_index("tok")
        self.col = lax.axis_index("col")
        self.z = self.tok // 2
        self.c = self.tok % 2
        self.x = self.col // NX
        self.y = self.col % NX
        self.sib = (self.zc(0, 1 - self.c), self.col)
        self.zn = ((self.zc(1, self.c), self.col), (self.zc(-1, self.c), self.col))

    def zc(self, dz, c):
        return ((self.z + dz + NZ) % NZ) * 2 + c

    def xy(self, dx, dy):
        return ((self.x + dx + NX) % NX) * NX + (self.y + dy + NX) % NX

    def peer(self, dx, dy):
        return (self.tok, self.xy(dx, dy))


def remote(src, dst, ssem, rsem, dev):
    return pltpu.make_async_remote_copy(
        src_ref=src, dst_ref=dst, send_sem=ssem, recv_sem=rsem, device_id=dev, device_id_type=MESH
    )


def greet(devices):
    barrier = pltpu.get_barrier_semaphore()
    for dev in devices:
        pl.semaphore_signal(barrier, inc=1, device_id=dev, device_id_type=MESH)
    pl.semaphore_wait(barrier, len(devices))


class Ring:
    def __init__(self, at, dst, rsend, rrecv, ssend, srecv, own):
        self.at, self.dst, self.own = at, dst, own
        self.ring, self.side = (rsend, rrecv), (ssend, srecv)
        self.sent = []

    def start(self, copy):
        copy.start()
        self.sent.append(copy)

    def block(self, d, h, s, core):
        return self.dst.at[pl.ds(self.at.zc(-s if d == 0 else s, core) * LOCAL + h * (LOCAL // 2), LOCAL // 2)]

    def hop(self, d, h, s):
        b = self.block(d, h, s, self.at.c)
        return remote(b, b, self.ring[0].at[d, h, s], self.ring[1].at[d, h, s], self.at.zn[d])

    def across(self, d, h, s, core):
        b = self.block(d, h, s, core)
        return remote(b, b, self.side[0].at[d, h, s - 1], self.side[1].at[d, h, s - 1], self.at.sib)

    def whole(self, core):
        b = self.dst.at[pl.ds(self.at.zc(0, core) * LOCAL, LOCAL)]
        return remote(b, b, self.own.at[0], self.own.at[1], self.at.sib)

    def begin(self):
        for h in range(2):
            for d in range(2):
                self.start(self.hop(d, h, 0))
        self.start(self.whole(self.at.c))

    def step(self, s, h):
        for d in range(2):
            if s > HOPS[d][h]:
                continue
            b = self.block(d, h, s, self.at.c)
            remote(b, b, self.ring[0].at[d, h, s - 1], self.ring[1].at[d, h, s - 1], self.at.zn[d]).wait_recv()
            if s < HOPS[d][h]:
                self.start(self.hop(d, h, s))
            self.start(self.across(d, h, s, self.at.c))

    def finish(self):
        other = 1 - self.at.c
        self.whole(other).wait_recv()
        for s in range(1, 9):
            for h in range(2):
                for d in range(2):
                    if s <= HOPS[d][h]:
                        self.across(d, h, s, other).wait_recv()

    def flush(self):
        for copy in self.sent:
            copy.wait_send()


def xy_gather(at, dst, n, cut, sends, recvs, first):
    sent = []
    lo, hi = pl.ds(0, cut), pl.ds(cut, n - cut)

    def shift(a, b):
        return (a, b) if first == 0 else (b, a)

    def dev(a, b):
        return at.peer(*shift(a, b))

    def slot(a, b):
        return dst.at[pl.ds(pl.multiple_of(at.xy(*shift(a, b)) * n, n), n)]

    def start(block, k, to):
        copy = remote(block, block, sends.at[k], recvs.at[k], to)
        copy.start()
        sent.append(copy)

    def wait(block, k, to):
        remote(block, block, sends.at[k], recvs.at[k], to).wait_recv()

    start(slot(0, 0), 0, dev(1, 0))
    start(slot(0, 0), 1, dev(-1, 0))
    start(slot(0, 0), 4, dev(0, 1))
    start(slot(0, 0), 5, dev(0, -1))
    yield
    wait(slot(-1, 0), 0, dev(1, 0))
    start(slot(-1, 0).at[lo], 2, dev(1, 0))
    wait(slot(1, 0), 1, dev(-1, 0))
    start(slot(1, 0).at[hi], 3, dev(-1, 0))
    for item, a in ((1, -1), (2, 1)):
        start(slot(a, 0), 4 + 4 * item, dev(0, 1))
        start(slot(a, 0), 5 + 4 * item, dev(0, -1))
    yield
    wait(slot(2, 0).at[lo], 2, dev(1, 0))
    wait(slot(2, 0).at[hi], 3, dev(-1, 0))
    start(slot(2, 0), 4 + 4 * 3, dev(0, 1))
    start(slot(2, 0), 5 + 4 * 3, dev(0, -1))
    yield
    for item, a in ((0, 0), (1, -1), (2, 1), (3, 2)):
        k = 4 + 4 * item
        wait(slot(a, -1), k, dev(0, 1))
        start(slot(a, -1).at[lo], k + 2, dev(0, 1))
        wait(slot(a, 1), k + 1, dev(0, -1))
        start(slot(a, 1).at[hi], k + 3, dev(0, -1))
        yield
    for item, a in ((0, 0), (1, -1), (2, 1), (3, 2)):
        k = 4 + 4 * item
        wait(slot(a, 2).at[lo], k + 2, dev(0, 1))
        wait(slot(a, 2).at[hi], k + 3, dev(0, -1))
    for copy in sent:
        copy.wait_send()


def xy_reduce(at, terms, n, first, waits, done, got1, part, got2, send1, recv1, send2, recv2):
    sent = []
    mine = (at.x, at.y) if first == 0 else (at.y, at.x)

    def dev(a, b):
        return at.peer(a, b) if first == 0 else at.peer(b, a)

    def line(i, size):
        return pl.ds(pl.multiple_of(((i + NX) % NX) * size, size), size)

    for k, a in enumerate((2, 1, -1)):
        copy = remote(terms.at[line(mine[0] + a, NX * n)], got1.at[k], send1.at[k], recv1.at[k], dev(a, 0))
        copy.start()
        sent.append(copy)
    for _ in range(waits[0]):
        yield
    for k, a in enumerate((2, 1, -1)):
        remote(got1.at[k], got1.at[k], send1.at[k], recv1.at[k], dev(a, 0)).wait_recv()

    def add(b, carry):
        v = terms[pl.ds(pl.multiple_of((mine[0] * NX + b) * n, n), n), :].astype(F32)
        rows = pl.ds(pl.multiple_of(b * n, n), n)
        for k in range(3):
            v = v + got1[k, rows, :].astype(F32)
        part[rows, :] = v.astype(part.dtype)
        return carry

    lax.fori_loop(0, NX, add, 0)
    for k, b in enumerate((2, 1, -1)):
        copy = remote(part.at[line(mine[1] + b, n)], got2.at[k], send2.at[k], recv2.at[k], dev(0, b))
        copy.start()
        sent.append(copy)
    for _ in range(waits[1]):
        yield
    for k, b in enumerate((2, 1, -1)):
        remote(got2.at[k], got2.at[k], send2.at[k], recv2.at[k], dev(0, b)).wait_recv()
    v = part[line(mine[1], n), :].astype(F32)
    for k in range(3):
        v = v + got2[k].astype(F32)
    done(v)
    for copy in sent:
        copy.wait_send()


def sub(h):
    return (0, 528, 176) if h == 0 else (528, 512, 128)


class RingSum:
    ORDER = (8, 7, -7, 6, -6, 5, -5, 4, -4, 3, -3, 2, -2, 1, -1, 0)

    def __init__(self, at, mine, theirs, stage, land, xsend, xrecv, rsend, rrecv):
        self.at, self.mine, self.theirs, self.stage, self.land = at, mine, theirs, stage, land
        self.side, self.ring = (xsend, xrecv), (rsend, rrecv)
        self.sent = []

    def give(self, off):
        copy = remote(
            self.mine.at[self.at.zc(off, 1 - self.at.c)],
            self.theirs.at[off + 7],
            self.side[0].at[off + 7],
            self.side[1].at[off + 7],
            self.at.sib,
        )
        copy.start()
        self.sent.append(copy)

    def wait_side(self, off):
        b = self.theirs.at[off + 7]
        remote(b, b, self.side[0].at[off + 7], self.side[1].at[off + 7], self.at.sib).wait_recv()

    def landed(self, d, h, s):
        first, size, tile = sub(h)
        b = self.land.at[d, s, pl.ds(first, size)]
        remote(b, b, self.ring[0].at[d, h, s], self.ring[1].at[d, h, s], self.at.zn[d]).wait_recv()

    def step(self, s, h):
        if h == 0:
            if s == 0:
                self.wait_side(8)
            if s < 7:
                self.wait_side(7 - s)
                self.wait_side(s - 7)
        first, size, tile = sub(h)
        for d in range(2):
            if s >= HOPS[d][h]:
                continue
            far = HOPS[d][h] - s
            off = far if d == 0 else -far
            buf = 8 if far == 8 else off
            owner = self.at.zc(off, self.at.c)
            if s:
                self.landed(d, h, s - 1)
            for t in range(size // tile):
                rows = pl.ds(first + t * tile, tile)
                v = self.mine[owner, rows, :].astype(F32) + self.theirs[buf + 7, rows, :].astype(F32)
                if s:
                    v = v + self.land[d, s - 1, rows, :].astype(F32)
                self.stage[d, s, rows, :] = v.astype(BF16)
            rows = pl.ds(first, size)
            copy = remote(
                self.stage.at[d, s, rows],
                self.land.at[d, s, rows],
                self.ring[0].at[d, h, s],
                self.ring[1].at[d, h, s],
                self.at.zn[d],
            )
            copy.start()
            self.sent.append(copy)

    def finish(self):
        self.wait_side(0)
        for h in range(2):
            for d in range(2):
                self.landed(d, h, HOPS[d][h] - 1)

    def total(self, rows, h):
        v = self.mine[self.at.tok, rows, :].astype(F32) + self.theirs[7, rows, :].astype(F32)
        for d in range(2):
            v = v + self.land[d, HOPS[d][h] - 1, rows, :].astype(F32)
        return v

    def flush(self):
        for copy in self.sent:
            copy.wait_send()


def dma(*shape):
    return pltpu.SemaphoreType.DMA(shape)


def vmem(dtype, *shape):
    return pltpu.VMEM(shape, dtype)


def by(gen, n):
    alive = True
    while alive:
        for _ in range(n):
            try:
                next(gen)
            except StopIteration:
                alive = False
                break
        if alive:
            yield


def joint(*gens):
    gens = list(gens)
    while gens:
        left = []
        for g in gens:
            try:
                next(g)
                left.append(g)
            except StopIteration:
                pass
        gens = left
        if gens:
            yield


RING_SEMS = [dma(2, 2, 8), dma(2, 2, 8), dma(2, 2, 8), dma(2, 2, 8), dma(2)]
RED_SEMS = [dma(3)] * 4

SCRATCH = dict(
    kbuf=[vmem(BF16, PAGES, PAGE, LANE)],
    vbuf=[vmem(BF16, PAGES, PAGE, LANE)],
    gbuf=[vmem(BF16, OWNERS, GROWS, LANE)],
    tbuf=[vmem(BF16, NCOL * HALF, LANE)] * 2,
    cbuf=[vmem(BF16, NCOL * HALF, LANE)] * 2,
    wqg=[vmem(BF16, KW, 2 * LANE)],
    qbuf=[vmem(BF16, ROWS, LANE)],
    act=[vmem(F32, ROWS, LANE)],
    grads=[vmem(BF16, NB, BLK, LANE)],
    gated=[vmem(BF16, ROWS, LANE)],
    scores=[vmem(F32, ROWS, 2 * LANE)] * 2,
    sums=[vmem(F32, SHARE, 2 * LANE)] * 2,
    wbuf=[vmem(BF16, ROWS, 2 * LANE)] * 2,
    wpick=[vmem(BF16, PAIRS, BLK, LANE)],
    sred_a=[vmem(F32, 3, NX * SHARE, 2 * LANE), vmem(F32, NX * SHARE, 2 * LANE), vmem(F32, 3, SHARE, 2 * LANE)] + RED_SEMS,
    sred_b=[vmem(F32, 3, NX * SHARE, 2 * LANE), vmem(F32, NX * SHARE, 2 * LANE), vmem(F32, 3, SHARE, 2 * LANE)] + RED_SEMS,
    ored_a=[vmem(BF16, 3, NX * HALF, LANE), vmem(BF16, NX * HALF, LANE), vmem(BF16, 3, HALF, LANE)] + RED_SEMS,
    ored_b=[vmem(BF16, 3, NX * HALF, LANE), vmem(BF16, NX * HALF, LANE), vmem(BF16, 3, HALF, LANE)] + RED_SEMS,
    gring=[
        vmem(BF16, NZ, GROWS, LANE),
        vmem(BF16, 2, 8, GROWS, LANE),
        vmem(BF16, 2, 8, GROWS, LANE),
        dma(16),
        dma(16),
        dma(2, 2, 8),
        dma(2, 2, 8),
    ],
    kring=RING_SEMS,
    vring=RING_SEMS,
    tsem=[dma(20)] * 4,
    csem=[dma(20)] * 4,
    wsem=[dma(20)] * 4,
)
NAMES = list(SCRATCH)
FLAT = [s for name in NAMES for s in SCRATCH[name]]


def kernel(pids, pair, block, mark, step_of, keys, tokens, cotangent, values, rate, wq, wg, wo, out, total, touched, *refs):
    refs = list(refs)
    s = {}
    for name in NAMES:
        n = len(SCRATCH[name])
        s[name], refs = refs[:n], refs[n:]
    (kbuf,), (vbuf,), (gbuf,), (wqg,), (qbuf,), (act,), (grads,), (gated,), (wpick,) = (
        s[n] for n in ("kbuf", "vbuf", "gbuf", "wqg", "qbuf", "act", "grads", "gated", "wpick")
    )
    at = Place()
    flags = set()
    greet([at.zn[0], at.zn[1], at.sib] + [at.peer(a, 0) for a in (1, -1, 2)] + [at.peer(0, a) for a in (1, -1, 2)])

    def factor(p):
        return jnp.exp(-(STEP - step_of[p]).astype(F32) * rate[...])

    kring = Ring(at, kbuf, *s["kring"])
    vring = Ring(at, vbuf, *s["vring"])
    gring = RingSum(at, gbuf, *s["gring"])

    def zchain():
        kbuf[pl.ds(at.tok * LOCAL, LOCAL)] = keys[...]
        kring.begin()
        for p in range(LOCAL):
            vbuf[at.tok * LOCAL + p] = (values[p] * factor(p)).astype(BF16)
        yield
        for step in range(1, 9):
            for h in range(2):
                kring.step(step, h)
                if (step, h) == (7, 1):
                    vring.begin()
                yield
        kring.finish()
        flags.add("keys")
        yield
        for step in range(1, 9):
            for h in range(2):
                vring.step(step, h)
                if step >= 7 and "grads" in flags and "begun" not in flags:
                    flags.add("begun")
                    gring.step(0, 0)
                    gring.step(0, 1)
                yield
        vring.finish()
        flags.add("values")
        while "grads" not in flags:
            yield
        if "begun" not in flags:
            gring.step(0, 0)
            gring.step(0, 1)
            yield
        for step in range(1, 8):
            for h in range(2):
                gring.step(step, h)
                yield
        gring.finish()

    def copy_in(src, bufs):
        rows = pl.ds(pl.multiple_of(at.col * HALF, HALF), HALF)
        for h in range(2):
            bufs[h][rows, :] = src[h * HALF : (h + 1) * HALF, :]

    def wide(buf, r):
        return jnp.concatenate(
            [buf[pl.ds(pl.multiple_of(k * HALF + r * 128, 128), 128), :] for k in range(NCOL)], axis=1
        )

    def forward():
        copy_in(tokens, s["tbuf"])
        copy_in(cotangent, s["cbuf"])
        gens = [xy_gather(at, s["tbuf"][f], HALF, 192, *s["tsem"][2 * f : 2 * f + 2], f) for f in range(2)]
        yield from joint(*gens)
        flags.add("tokens")
        wqg[:, :LANE] = wq[...]
        wqg[:, LANE:] = wg[...]
        for h in range(2):

            def tile(r, carry, h=h):
                both = jnp.dot(wide(s["tbuf"][h], r), wqg[...], preferred_element_type=F32)
                rows = pl.ds(pl.multiple_of(h * HALF + r * 128, 128), 128)
                qbuf[rows, :] = both[:, :LANE].astype(BF16)
                g = both[:, LANE:]
                act[rows, :] = g / (1.0 + jnp.exp(-g))
                return carry

            lax.fori_loop(0, 3, tile, 0)
            yield
        flags.add("queries")

    def backward():
        for _ in range(6):
            yield
        gens = [xy_gather(at, s["cbuf"][f], HALF, 192, *s["csem"][2 * f : 2 * f + 2], f) for f in range(2)]
        yield from joint(*gens)
        while "queries" not in flags:
            yield
        for h in range(2):

            def tile(r, carry, h=h):
                g = lax.dot_general(
                    wide(s["cbuf"][h], r), wo[...], (((1,), (1,)), ((), ())), preferred_element_type=F32
                )
                rows = pl.ds(pl.multiple_of(h * HALF + r * 128, 128), 128)
                g = (g * act[rows, :]).astype(BF16)
                grads[h * (NB // 2) + 2 * r] = g[:BLK]
                grads[h * (NB // 2) + 2 * r + 1] = g[BLK:]
                return carry

            lax.fori_loop(0, 3, tile, 0)
            yield
        flags.add("backward")

    def lookup():
        while not {"keys", "queries"} <= flags:
            yield
        for b in range(NB):
            q = qbuf[b * BLK : (b + 1) * BLK, :]
            for i in range(PICKS):
                page = kbuf[pids[b * PICKS + i]]
                v = lax.dot_general(q, page, (((1,), (1,)), ((), ())), preferred_element_type=F32)
                lanes = slice((i % 2) * PAGE, (i % 2 + 1) * PAGE)
                r = 0
                while r < BLK:
                    row = b * BLK + r
                    j, o = row // SHARE, row % SHARE
                    size = min(SHARE - o, BLK - r)
                    spot = j if i < 2 else (j % NX) * NX + j // NX
                    s["scores"][i // 2][spot * SHARE + o : spot * SHARE + o + size, lanes] = v[r : r + size]
                    r += size
            if b % 6 == 5:
                yield

        def keep(f):
            def done(v):
                s["sums"][f][...] = v * (KW**-0.5)

            return done

        gens = [
            xy_reduce(at, s["scores"][f], SHARE, f, (3, 1), keep(f), *s["sred_b" if f else "sred_a"]) for f in range(2)
        ]
        yield from joint(*gens)
        left, right = s["sums"][0][...], s["sums"][1][...]
        top = jnp.maximum(jnp.max(left, axis=1, keepdims=True), jnp.max(right, axis=1, keepdims=True))
        left, right = jnp.exp(left - top), jnp.exp(right - top)
        total = jnp.sum(left, axis=1, keepdims=True) + jnp.sum(right, axis=1, keepdims=True)
        rows = pl.ds(pl.multiple_of(at.col * SHARE, SHARE), SHARE)
        s["wbuf"][0][rows, :] = (left / total).astype(BF16)
        s["wbuf"][1][rows, :] = (right / total).astype(BF16)
        gens = [xy_gather(at, s["wbuf"][f], SHARE, 16 + 16 * f, *s["wsem"][2 * f : 2 * f + 2], f) for f in range(2)]
        yield from by(joint(*gens), 3)
        for b in range(NB):
            for i in range(PICKS):
                lanes = slice((i % 2) * PAGE, (i % 2 + 1) * PAGE)
                wpick[b * PICKS + i] = s["wbuf"][i // 2][b * BLK : (b + 1) * BLK, lanes]
        flags.add("weights")
        while "backward" not in flags:
            yield
        for off in RingSum.ORDER:
            for core in range(2):
                owner = at.zc(off, core)
                found = []
                for k in range(2):
                    n = owner * 2 + k
                    v = lax.dot_general(
                        wpick[pair[n]], grads[block[n]], (((0,), (0,)), ((), ())), preferred_element_type=F32
                    )
                    found.append((v, [mark[n * LOCAL + p] for p in range(LOCAL)]))
                row = lax.broadcasted_iota(jnp.int32, (CNT, LANE), 0)
                count = jnp.zeros((CNT, LANE), F32)
                for p in range(LOCAL):
                    v = found[0][0] * found[0][1][p] + found[1][0] * found[1][1][p]
                    gbuf[owner, p * PAGE : (p + 1) * PAGE, :] = v.astype(BF16)
                    count = jnp.where(row == p, found[0][1][p] + found[1][1][p], count)
                gbuf[owner, OWN:, :] = count.astype(BF16)
            gring.give(off)
            if off in (-7, -5, -3, -1):
                yield
        flags.add("grads")
        yield
        while "values" not in flags:
            yield

        def mix(b, carry):
            rows = pl.ds(pl.multiple_of(b * BLK, BLK), BLK)
            m = jnp.zeros((BLK, LANE), F32)
            for i in range(PICKS):
                n = b * PICKS + i
                m += jnp.dot(wpick[n], vbuf[pids[n]], preferred_element_type=F32)
            gated[rows, :] = (m * act[rows, :]).astype(BF16)
            return carry

        lax.fori_loop(0, NB, mix, 0)
        yield
        for k in range(NCOL):
            o = jnp.dot(gated[...], wo[:, k * LANE : (k + 1) * LANE], preferred_element_type=F32).astype(BF16)
            turned = (k % NX) * NX + k // NX
            s["tbuf"][0][k * HALF : (k + 1) * HALF, :] = o[:HALF]
            s["tbuf"][1][turned * HALF : (turned + 1) * HALF, :] = o[HALF:]
            if k % 8 == 7:
                yield

        def give(f):
            def done(v):
                out[f * HALF : (f + 1) * HALF, :] = v.astype(BF16)

            return done

        gens = [xy_reduce(at, s["tbuf"][f], HALF, f, (7, 2), give(f), *s["ored_b" if f else "ored_a"]) for f in range(2)]
        yield from joint(*gens)

    for _ in joint(zchain(), forward(), backward(), lookup()):
        pass
    touched[...] = gring.total(pl.ds(OWN, CNT), 1)
    for h, lo, hi in ((0, 0, 528), (1, 528, OWN)):
        for a in range(lo, hi, 16):
            rows = pl.ds(a, 16)
            total[rows, :] = gring.total(rows, h)
    kring.flush()
    vring.flush()
    gring.flush()


def settle_kernel(step_of, rate, raw, total, touched, values, momentum, out, new_values, new_momentum):
    out[...] = raw[...]
    for p in range(LOCAL):
        f = jnp.exp(-(STEP - step_of[p]).astype(F32) * rate[...])
        hit = touched[p : p + 1, :] > 0.5
        v, m = values[p], momentum[p]
        m = jnp.where(hit, MOMENTUM_RATE * m + total[p] * f, m)
        new_momentum[p] = m
        new_values[p] = jnp.where(hit, v * f - LEARN_RATE * m, v)


def per_device(
    tokens,
    cotangent,
    query_weight,
    slot_keys,
    values,
    momentum,
    page_ids,
    last_step,
    decay_rate,
    gate_weight,
    out_weight,
):
    pids = page_ids.reshape(-1)
    match = (pids // LOCAL)[None, :] == jnp.arange(OWNERS)[:, None]
    code = (jnp.arange(PAIRS) * LOCAL + pids % LOCAL)[None, :]
    none = PAIRS * LOCAL
    first = jnp.min(jnp.where(match, code, none), axis=1)
    last = jnp.max(jnp.where(match, code, -1), axis=1)
    both = jnp.stack([first, last], axis=1)
    valid = jnp.stack([first < none, last > first], axis=1)
    both = jnp.where(valid, both, 0)
    pair = (both // LOCAL).reshape(-1)
    mark = (valid[:, :, None] & ((both % LOCAL)[:, :, None] == jnp.arange(LOCAL))).astype(F32).reshape(-1)
    paged = (LOCAL, PAGE, LANE)
    rate = decay_rate.reshape(1, LANE)
    stored = values.reshape(paged)
    raw, total, touched = pl.pallas_call(
        kernel,
        out_shape=(
            jax.ShapeDtypeStruct((ROWS, LANE), BF16),
            jax.ShapeDtypeStruct((OWN, LANE), F32),
            jax.ShapeDtypeStruct((CNT, LANE), F32),
        ),
        in_specs=[SM] * 5 + [VM] * 8,
        out_specs=(VM,) * 3,
        scratch_shapes=FLAT,
        compiler_params=pltpu.CompilerParams(collective_id=0, has_side_effects=True, vmem_limit_bytes=60 << 20),
    )(
        pids,
        pair,
        pair // PICKS,
        mark,
        last_step,
        slot_keys.reshape(paged),
        tokens,
        cotangent,
        stored,
        rate,
        query_weight,
        gate_weight,
        out_weight,
    )
    layer_out, new_values, new_momentum = pl.pallas_call(
        settle_kernel,
        out_shape=(
            jax.ShapeDtypeStruct((ROWS, LANE), BF16),
            jax.ShapeDtypeStruct(paged, F32),
            jax.ShapeDtypeStruct(paged, F32),
        ),
        in_specs=[SM] + [VM] * 6,
        out_specs=(VM,) * 3,
    )(last_step, rate, raw, total.reshape(paged), touched, stored, momentum.reshape(paged))
    return (layer_out, new_values.reshape(OWN, LANE), new_momentum.reshape(OWN, LANE))


def solution(mesh):
    in_specs = (
        P("tok", "col"),
        P("tok", "col"),
        P(None, "col"),
        P("tok", "col"),
        P("tok", "col"),
        P("tok", "col"),
        P("tok", None),
        P("tok"),
        P("col"),
        P(None, "col"),
        P("col", None),
    )
    out_specs = (P("tok", "col"), P("tok", "col"), P("tok", "col"))
    return jax.shard_map(
        per_device, mesh=mesh, in_specs=in_specs, out_specs=out_specs, check_vma=False
    )
```

time: 491 us -> 175 us (0.36); the launches traced: 485 us -> 175 us
  waiting for transfers between devices: 240 us -> 0 us
  Pallas kernels: 0 us -> 171 us
  blocking collectives: 159 us -> 0 us
  starting transfers between devices: 24.3 us -> 0 us
  local copies, waits for them, and re-layouts: 22.4 us -> 2.41 us
  matrix products: 16.6 us -> 0 us
  between operations: 14.3 us -> 0.68 us
  other arithmetic: 8.47 us -> 0.82 us
    all_to_all x4 -> x0, waiting for transfers between devices: 240 us -> none  [the longest x1 99.2 us: per_device(): lax.all_to_all(reply_keys, 'tok', split_axis=0, concat_axis=0, tiled=True)]
    pallas_call x0 -> x2, Pallas kernels: none -> 171 us  [the longest x1 168 us: per_device(): pl.pallas_call(kernel, out_shape=(jax.ShapeDtypeStruct((ROWS, LANE), BF16...]
    all_to_all x3 -> x0, blocking collectives: 159 us -> none  [the longest x1 106 us: per_device(): lax.all_to_all(reply_values, 'tok', split_axis=0, concat_axis=0, tiled=True)]
    all_to_all x4 -> x0, starting transfers between devices: 24.3 us -> none  [the longest x1 10.9 us: per_device(): lax.all_to_all(outgoing.reshape(owners, capacity, page_slots, col_width),...]
    dot_general x8 -> x0, matrix products: 16.6 us -> none  [the longest x1 3.74 us: per_device(): jnp.dot(page_match.astype(jnp.bfloat16), returned.reshape(send_slots, pag...]
    scatter x1 -> x0, local copies, waits for them, and re-layouts: 6.62 us -> none  [per_device(): outgoing.at[send_slot]]
    gather x4 -> x0, local copies, waits for them, and re-layouts: 5.81 us -> none  [the longest x1 1.96 us: per_device(): got_values.reshape(send_slots, page_slots, col_width)[send_slot]]
  transfers between devices with their start and end apart: 5 -> 0, of which waited for: 4 -> 0; matrix products, arithmetic and copies ran while one was open for 3% -> 0% of each run, Pallas kernels for 0% -> 0%
where the time goes in v2:
time: 175 us
  Pallas kernels  171 us (98%)
  local copies, waits for them, and re-layouts  2.41 us (1%)
    pallas_call x1, Pallas kernels, per_device(): pl.pallas_call(kernel, out_shape=(jax.ShapeDtypeStruct((ROWS, LANE), BF16...  168 us

profile of v2, /device:TPU:1, one launch (start us, length us, event | category | flops | bytes accessed | tf_op | source)
XLA Modules:
  0.0 174.6 jit_solution(16617754151941667301)
XLA Ops:
  0.6 0.0 copy-start.1
  0.6 0.7 copy-done.1
  1.3 0.1 copy.22
  1.4 0.1 reshape.161.pids
  1.5 0.0 copy-start
  1.5 0.5 copy-done
  2.0 0.1 select_reduce_fusion.1
  2.2 0.1 copy.24
  2.3 0.1 copy.25
  2.4 0.1 and_convert_fusion
  2.5 0.7 reshape.168.mark
  3.2 0.1 copy.23
  3.3 0.1 select_n.65
  3.4 0.5 and_select_fusion.1
  3.9 168.1 %shard_map.130 = (bf16[768,128]{1,0:T(8,128)(2,1)}, f32[1024,128]{1,0:T(8,128)}, f32[16,128]{1,0:T(8,128)}) custom-call(s32[48]{0:T(128)} %copy-done, s32[64]{0:T(128)} %get-tuple-element.21.pair, s32[64]{0:T(128)} %get-tuple-element.20.block, f32[512]{0:T(512)} %reshape.168.mark, s32[8]{0:T(128)} %step_of.3, bf16[8,128,128]{2,1,0:T(8,128)(2,1)} %bitcast.16, ...), custom_call_target="tpu_custom_call" | custom-call | tf_op jit(solution)/shard_map/pallas_call | solution.py:647
  172.0 2.6 %shard_map.131 = (bf16[768,128]{1,0:T(8,128)(2,1)}, f32[8,128,128]{2,1,0:T(8,128)}, f32[8,128,128]{2,1,0:T(8,128)}) custom-call(s32[8]{0:T(128)} %step_of.3, f32[1,128]{1,0:T(1,128)} %bitcast.20, bf16[768,128]{1,0:T(8,128)(2,1)} %get-tuple-element.9.raw, f32[8,128,128]{2,1,0:T(8,128)} %bitcast.15, f32[16,128]{1,0:T(8,128)} %get-tuple-element.11.touched, ...), custom_call_target="tpu_custom_call" | custom-call | tf_op jit(solution)/shard_map/pallas_call | solution.py:673
  (3 shorter events, 0.0 us)
Async XLA Ops:
  0.6 0.7 copy-start.1
  1.5 0.5 copy-start

commit v3 on v2

--- a/solution.py
+++ b/solution.py
@@ -28,9 +28,14 @@
 HALF = ROWS // 2
 CNT = 16
 GROWS = OWN + CNT
+TSTART = 3
+TPACE = ()
+CSTART = 8
+CPACE = (3,)
 MESH = pl.DeviceIdType.MESH
 HOPS = ((8, 7), (7, 8))
 VM = pl.BlockSpec(memory_space=pltpu.VMEM)
+ANY = pl.BlockSpec(memory_space=pl.ANY)
 SM = pl.BlockSpec(memory_space=pltpu.SMEM)
 F32 = jnp.float32
 BF16 = jnp.bfloat16
@@ -71,8 +76,8 @@
 
 
 class Ring:
-    def __init__(self, at, dst, rsend, rrecv, ssend, srecv, own):
-        self.at, self.dst, self.own = at, dst, own
+    def __init__(self, at, src, dst, rsend, rrecv, ssend, srecv, own):
+        self.at, self.src, self.dst, self.own = at, src, dst, own
         self.ring, self.side = (rsend, rrecv), (ssend, srecv)
         self.sent = []
 
@@ -85,21 +90,23 @@
 
     def hop(self, d, h, s):
         b = self.block(d, h, s, self.at.c)
-        return remote(b, b, self.ring[0].at[d, h, s], self.ring[1].at[d, h, s], self.at.zn[d])
+        from_ = b if s else self.src.at[pl.ds(h * (LOCAL // 2), LOCAL // 2)]
+        return remote(from_, b, self.ring[0].at[d, h, s], self.ring[1].at[d, h, s], self.at.zn[d])
 
     def across(self, d, h, s, core):
         b = self.block(d, h, s, core)
         return remote(b, b, self.side[0].at[d, h, s - 1], self.side[1].at[d, h, s - 1], self.at.sib)
 
-    def whole(self, core):
-        b = self.dst.at[pl.ds(self.at.zc(0, core) * LOCAL, LOCAL)]
+    def whole(self):
+        b = self.dst.at[pl.ds(self.at.zc(0, 1 - self.at.c) * LOCAL, LOCAL)]
         return remote(b, b, self.own.at[0], self.own.at[1], self.at.sib)
 
     def begin(self):
         for h in range(2):
             for d in range(2):
                 self.start(self.hop(d, h, 0))
-        self.start(self.whole(self.at.c))
+        b = self.dst.at[pl.ds(self.at.tok * LOCAL, LOCAL)]
+        self.start(remote(self.src, b, self.own.at[0], self.own.at[1], self.at.sib))
 
     def step(self, s, h):
         for d in range(2):
@@ -113,7 +120,7 @@
 
     def finish(self):
         other = 1 - self.at.c
-        self.whole(other).wait_recv()
+        self.whole().wait_recv()
         for s in range(1, 9):
             for h in range(2):
                 for d in range(2):
@@ -125,7 +132,7 @@
             copy.wait_send()
 
 
-def xy_gather(at, dst, n, cut, sends, recvs, first):
+def xy_gather(at, src, dst, n, cut, sends, recvs, first):
     sent = []
     lo, hi = pl.ds(0, cut), pl.ds(cut, n - cut)
 
@@ -146,10 +153,10 @@
     def wait(block, k, to):
         remote(block, block, sends.at[k], recvs.at[k], to).wait_recv()
 
-    start(slot(0, 0), 0, dev(1, 0))
-    start(slot(0, 0), 1, dev(-1, 0))
-    start(slot(0, 0), 4, dev(0, 1))
-    start(slot(0, 0), 5, dev(0, -1))
+    for k, to in ((0, dev(1, 0)), (1, dev(-1, 0)), (4, dev(0, 1)), (5, dev(0, -1))):
+        copy = remote(src, slot(0, 0), sends.at[k], recvs.at[k], to)
+        copy.start()
+        sent.append(copy)
     yield
     wait(slot(-1, 0), 0, dev(1, 0))
     start(slot(-1, 0).at[lo], 2, dev(1, 0))
@@ -175,6 +182,45 @@
         k = 4 + 4 * item
         wait(slot(a, 2).at[lo], k + 2, dev(0, 1))
         wait(slot(a, 2).at[hi], k + 3, dev(0, -1))
+    for copy in sent:
+        copy.wait_send()
+
+
+def xy_spread(at, dst, n, sends, recvs, first, waits):
+    sent = []
+
+    def dev(a, b):
+        return at.peer(a, b) if first == 0 else at.peer(b, a)
+
+    def slot(a, b):
+        i = at.xy(a, b) if first == 0 else at.xy(b, a)
+        return dst.at[pl.ds(pl.multiple_of(i * n, n), n)]
+
+    def start(block, k, to):
+        copy = remote(block, block, sends.at[k], recvs.at[k], to)
+        copy.start()
+        sent.append(copy)
+
+    def wait(block, k, to):
+        remote(block, block, sends.at[k], recvs.at[k], to).wait_recv()
+
+    line = (2, 1, -1)
+    for k, a in enumerate(line):
+        start(slot(0, 0), k, dev(a, 0))
+    for k, b in enumerate(line):
+        start(slot(0, 0), 3 + k, dev(0, b))
+    for _ in range(waits[0]):
+        yield
+    for j, a in enumerate(line):
+        wait(slot(-a, 0), j, dev(a, 0))
+        for k, b in enumerate(line):
+            start(slot(-a, 0), 6 + 3 * j + k, dev(0, b))
+    for _ in range(waits[1]):
+        yield
+    for k, b in enumerate(line):
+        wait(slot(0, -b), 3 + k, dev(0, b))
+        for j, a in enumerate(line):
+            wait(slot(-a, -b), 6 + 3 * j + k, dev(0, b))
     for copy in sent:
         copy.wait_send()
 
@@ -314,16 +360,9 @@
     return pltpu.VMEM(shape, dtype)
 
 
-def by(gen, n):
-    alive = True
-    while alive:
-        for _ in range(n):
-            try:
-                next(gen)
-            except StopIteration:
-                alive = False
-                break
-        if alive:
+def paced(gen, waits):
+    for i, _ in enumerate(gen):
+        for _ in range(waits[i] if i < len(waits) else 1):
             yield
 
 
@@ -352,6 +391,10 @@
     tbuf=[vmem(BF16, NCOL * HALF, LANE)] * 2,
     cbuf=[vmem(BF16, NCOL * HALF, LANE)] * 2,
     wqg=[vmem(BF16, KW, 2 * LANE)],
+    wobuf=[vmem(BF16, LANE, KW)],
+    wot=[vmem(BF16, KW, LANE)],
+    stored=[vmem(F32, LOCAL, PAGE, LANE)],
+    local=[dma(10)],
     qbuf=[vmem(BF16, ROWS, LANE)],
     act=[vmem(F32, ROWS, LANE)],
     grads=[vmem(BF16, NB, BLK, LANE)],
@@ -377,7 +420,7 @@
     vring=RING_SEMS,
     tsem=[dma(20)] * 4,
     csem=[dma(20)] * 4,
-    wsem=[dma(20)] * 4,
+    wsem=[dma(15)] * 4,
 )
 NAMES = list(SCRATCH)
 FLAT = [s for name in NAMES for s in SCRATCH[name]]
@@ -389,9 +432,10 @@
     for name in NAMES:
         n = len(SCRATCH[name])
         s[name], refs = refs[:n], refs[n:]
-    (kbuf,), (vbuf,), (gbuf,), (wqg,), (qbuf,), (act,), (grads,), (gated,), (wpick,) = (
-        s[n] for n in ("kbuf", "vbuf", "gbuf", "wqg", "qbuf", "act", "grads", "gated", "wpick")
+    (kbuf,), (vbuf,), (gbuf,), (wqg,), (qbuf,), (act,), (grads,), (gated,), (wpick,), (local,) = (
+        s[n] for n in ("kbuf", "vbuf", "gbuf", "wqg", "qbuf", "act", "grads", "gated", "wpick", "local")
     )
+    (wobuf,), (wot,), (stored,) = s["wobuf"], s["wot"], s["stored"]
     at = Place()
     flags = set()
     greet([at.zn[0], at.zn[1], at.sib] + [at.peer(a, 0) for a in (1, -1, 2)] + [at.peer(0, a) for a in (1, -1, 2)])
@@ -399,15 +443,23 @@
     def factor(p):
         return jnp.exp(-(STEP - step_of[p]).astype(F32) * rate[...])
 
-    kring = Ring(at, kbuf, *s["kring"])
-    vring = Ring(at, vbuf, *s["vring"])
+    mine = pl.ds(at.tok * LOCAL, LOCAL)
+    kring = Ring(at, keys, kbuf, *s["kring"])
+    vring = Ring(at, vbuf.at[mine], vbuf, *s["vring"])
+    places = pl.ds(pl.multiple_of(at.col * HALF, HALF), HALF)
+
+    def fetch(k, src, dst):
+        copy = pltpu.make_async_copy(src, dst, local.at[k])
+        copy.start()
+        return copy
+
+    halves = (pl.ds(0, HALF), pl.ds(HALF, HALF))
     gring = RingSum(at, gbuf, *s["gring"])
 
     def zchain():
-        kbuf[pl.ds(at.tok * LOCAL, LOCAL)] = keys[...]
         kring.begin()
-        for p in range(LOCAL):
-            vbuf[at.tok * LOCAL + p] = (values[p] * factor(p)).astype(BF16)
+        yield
+        got = fetch(0, keys, kbuf.at[mine]), fetch(1, values, stored)
         yield
         for step in range(1, 9):
             for h in range(2):
@@ -415,49 +467,60 @@
                 if (step, h) == (7, 1):
                     vring.begin()
                 yield
+                if (step, h) == (2, 0):
+                    for copy in got:
+                        copy.wait()
+                    for p in range(LOCAL):
+                        vbuf[at.tok * LOCAL + p] = (stored[p] * factor(p)).astype(BF16)
         kring.finish()
         flags.add("keys")
         yield
         for step in range(1, 9):
             for h in range(2):
                 vring.step(step, h)
-                if step >= 7 and "grads" in flags and "begun" not in flags:
+                if step >= 7 and 7 in flags and "begun" not in flags:
                     flags.add("begun")
                     gring.step(0, 0)
                     gring.step(0, 1)
                 yield
         vring.finish()
         flags.add("values")
-        while "grads" not in flags:
+        while 7 not in flags:
             yield
         if "begun" not in flags:
             gring.step(0, 0)
             gring.step(0, 1)
             yield
         for step in range(1, 8):
+            while 7 - step not in flags:
+                yield
             for h in range(2):
                 gring.step(step, h)
                 yield
         gring.finish()
 
-    def copy_in(src, bufs):
-        rows = pl.ds(pl.multiple_of(at.col * HALF, HALF), HALF)
-        for h in range(2):
-            bufs[h][rows, :] = src[h * HALF : (h + 1) * HALF, :]
-
     def wide(buf, r):
         return jnp.concatenate(
             [buf[pl.ds(pl.multiple_of(k * HALF + r * 128, 128), 128), :] for k in range(NCOL)], axis=1
         )
 
     def forward():
-        copy_in(tokens, s["tbuf"])
-        copy_in(cotangent, s["cbuf"])
-        gens = [xy_gather(at, s["tbuf"][f], HALF, 192, *s["tsem"][2 * f : 2 * f + 2], f) for f in range(2)]
-        yield from joint(*gens)
+        gens = [
+            xy_gather(at, tokens.at[halves[f]], s["tbuf"][f], HALF, 192, *s["tsem"][2 * f : 2 * f + 2], f) for f in range(2)
+        ]
+        gathered = joint(*gens)
+        next(gathered)
+        got = [fetch(2 + f, tokens.at[halves[f]], s["tbuf"][f].at[places]) for f in range(2)]
+        got.append(fetch(4, wq, wqg.at[:, pl.ds(0, LANE)]))
+        got.append(fetch(5, wg, wqg.at[:, pl.ds(LANE, LANE)]))
+        got.append(fetch(6, wo, wobuf))
+        got += [fetch(7 + f, cotangent.at[halves[f]], s["cbuf"][f].at[places]) for f in range(2)]
+        for _ in range(TSTART):
+            yield
+        yield from paced(gathered, TPACE)
+        for copy in got:
+            copy.wait()
         flags.add("tokens")
-        wqg[:, :LANE] = wq[...]
-        wqg[:, LANE:] = wg[...]
         for h in range(2):
 
             def tile(r, carry, h=h):
@@ -468,31 +531,33 @@
                 act[rows, :] = g / (1.0 + jnp.exp(-g))
                 return carry
 
-            lax.fori_loop(0, 3, tile, 0)
-            yield
+            for r in range(3):
+                lax.fori_loop(r, r + 1, tile, 0)
+                yield
+        wot[...] = wobuf[...].T
+        yield
         flags.add("queries")
 
     def backward():
-        for _ in range(6):
-            yield
-        gens = [xy_gather(at, s["cbuf"][f], HALF, 192, *s["csem"][2 * f : 2 * f + 2], f) for f in range(2)]
-        yield from joint(*gens)
+        for _ in range(CSTART):
+            yield
+        gens = [xy_gather(at, cotangent.at[halves[f]], s["cbuf"][f], HALF, 192, *s["csem"][2 * f : 2 * f + 2], f) for f in range(2)]
+        yield from paced(joint(*gens), CPACE)
         while "queries" not in flags:
             yield
         for h in range(2):
 
             def tile(r, carry, h=h):
-                g = lax.dot_general(
-                    wide(s["cbuf"][h], r), wo[...], (((1,), (1,)), ((), ())), preferred_element_type=F32
-                )
+                g = jnp.dot(wide(s["cbuf"][h], r), wot[...], preferred_element_type=F32)
                 rows = pl.ds(pl.multiple_of(h * HALF + r * 128, 128), 128)
                 g = (g * act[rows, :]).astype(BF16)
                 grads[h * (NB // 2) + 2 * r] = g[:BLK]
                 grads[h * (NB // 2) + 2 * r + 1] = g[BLK:]
                 return carry
 
-            lax.fori_loop(0, 3, tile, 0)
-            yield
+            for lo, hi in ((0, 2), (2, 3)):
+                lax.fori_loop(lo, hi, tile, 0)
+                yield
         flags.add("backward")
 
     def lookup():
@@ -532,8 +597,8 @@
         rows = pl.ds(pl.multiple_of(at.col * SHARE, SHARE), SHARE)
         s["wbuf"][0][rows, :] = (left / total).astype(BF16)
         s["wbuf"][1][rows, :] = (right / total).astype(BF16)
-        gens = [xy_gather(at, s["wbuf"][f], SHARE, 16 + 16 * f, *s["wsem"][2 * f : 2 * f + 2], f) for f in range(2)]
-        yield from by(joint(*gens), 3)
+        gens = [xy_spread(at, s["wbuf"][f], SHARE, *s["wsem"][2 * f : 2 * f + 2], f, (2, 2)) for f in range(2)]
+        yield from joint(*gens)
         for b in range(NB):
             for i in range(PICKS):
                 lanes = slice((i % 2) * PAGE, (i % 2 + 1) * PAGE)
@@ -559,10 +624,10 @@
                     count = jnp.where(row == p, found[0][1][p] + found[1][1][p], count)
                 gbuf[owner, OWN:, :] = count.astype(BF16)
             gring.give(off)
-            if off in (-7, -5, -3, -1):
-                yield
-        flags.add("grads")
-        yield
+            if off <= 0:
+                flags.add(-off)
+                if off in (-7, -5, -3, -1, 0):
+                    yield
         while "values" not in flags:
             yield
 
@@ -575,10 +640,11 @@
             gated[rows, :] = (m * act[rows, :]).astype(BF16)
             return carry
 
-        lax.fori_loop(0, NB, mix, 0)
-        yield
+        for b in (0, 6):
+            lax.fori_loop(b, b + 6, mix, 0)
+            yield
         for k in range(NCOL):
-            o = jnp.dot(gated[...], wo[:, k * LANE : (k + 1) * LANE], preferred_element_type=F32).astype(BF16)
+            o = jnp.dot(gated[...], wobuf[:, k * LANE : (k + 1) * LANE], preferred_element_type=F32).astype(BF16)
             turned = (k % NX) * NX + k // NX
             s["tbuf"][0][k * HALF : (k + 1) * HALF, :] = o[:HALF]
             s["tbuf"][1][turned * HALF : (turned + 1) * HALF, :] = o[HALF:]
@@ -591,7 +657,7 @@
 
             return done
 
-        gens = [xy_reduce(at, s["tbuf"][f], HALF, f, (7, 2), give(f), *s["ored_b" if f else "ored_a"]) for f in range(2)]
+        gens = [xy_reduce(at, s["tbuf"][f], HALF, f, (8, 3), give(f), *s["ored_b" if f else "ored_a"]) for f in range(2)]
         yield from joint(*gens)
 
     for _ in joint(zchain(), forward(), backward(), lookup()):
@@ -631,16 +697,21 @@
     out_weight,
 ):
     pids = page_ids.reshape(-1)
-    match = (pids // LOCAL)[None, :] == jnp.arange(OWNERS)[:, None]
     code = (jnp.arange(PAIRS) * LOCAL + pids % LOCAL)[None, :]
     none = PAIRS * LOCAL
-    first = jnp.min(jnp.where(match, code, none), axis=1)
-    last = jnp.max(jnp.where(match, code, -1), axis=1)
-    both = jnp.stack([first, last], axis=1)
-    valid = jnp.stack([first < none, last > first], axis=1)
-    both = jnp.where(valid, both, 0)
-    pair = (both // LOCAL).reshape(-1)
-    mark = (valid[:, :, None] & ((both % LOCAL)[:, :, None] == jnp.arange(LOCAL))).astype(F32).reshape(-1)
+
+    def listed(owner, second):
+        match = (pids // LOCAL)[None, :] == owner[:, None]
+        first = jnp.min(jnp.where(match, code, none), axis=1)
+        last = jnp.max(jnp.where(match, code, -1), axis=1)
+        valid = jnp.where(second, last > first, first < none)
+        return jnp.where(valid, jnp.where(second, last, first), 0), valid
+
+    n = jnp.arange(2 * OWNERS)
+    pair = listed(n // 2, n % 2 == 1)[0] // LOCAL
+    n = jnp.arange(2 * OWNERS * LOCAL)
+    both, valid = listed(n // (2 * LOCAL), n // LOCAL % 2 == 1)
+    mark = (valid & (both % LOCAL == n % LOCAL)).astype(F32)
     paged = (LOCAL, PAGE, LANE)
     rate = decay_rate.reshape(1, LANE)
     stored = values.reshape(paged)
@@ -651,7 +722,7 @@
             jax.ShapeDtypeStruct((OWN, LANE), F32),
             jax.ShapeDtypeStruct((CNT, LANE), F32),
         ),
-        in_specs=[SM] * 5 + [VM] * 8,
+        in_specs=[SM] * 5 + [ANY] * 4 + [VM] + [ANY] * 3,
         out_specs=(VM,) * 3,
         scratch_shapes=FLAT,
         compiler_params=pltpu.CompilerParams(collective_id=0, has_side_effects=True, vmem_limit_bytes=60 << 20),

time: 175 us -> 167 us (0.954)
  Pallas kernels: 171 us -> 164 us
    pallas_call x1, Pallas kernels: 168 us -> 161 us  [per_device(): pl.pallas_call(kernel, out_shape=(jax.ShapeDtypeStruct((ROWS, LANE), BF16...]
where the time goes in v3:
time: 167 us
  Pallas kernels  164 us (98%)
    pallas_call x1, Pallas kernels, per_device(): pl.pallas_call(kernel, out_shape=(jax.ShapeDtypeStruct((ROWS, LANE), BF16...  161 us

profile of v3, /device:TPU:1, one launch (start us, length us, event | category | flops | bytes accessed | tf_op | source)
XLA Modules:
  0.0 166.9 jit_solution(13735346113190823321)
XLA Ops:
  0.6 0.0 copy-start.1
  0.7 0.7 copy-done.1
  1.3 0.1 copy.16
  1.4 0.1 reshape.111.pids
  1.5 0.0 copy-start
  1.5 0.5 copy-done
  2.0 0.1 fusion.3
  2.1 0.5 and_select_fusion
  2.6 0.1 fusion.1
  2.7 0.6 and_convert_fusion.mark
  3.3 160.9 %shard_map.130 = (bf16[768,128]{1,0:T(8,128)(2,1)}, f32[1024,128]{1,0:T(8,128)}, f32[16,128]{1,0:T(8,128)}) custom-call(s32[48]{0:T(128)} %copy-done, s32[64]{0:T(128)} %get-tuple-element.20.pair, s32[64]{0:T(128)} %get-tuple-element.19.block, f32[512]{0:T(512)} %and_convert_fusion.mark, s32[8]{0:T(128)} %step_of.3, bf16[8,128,128]{2,1,0:T(8,128)(2,1)} %bitcast.11, ...), custom_call_target="tpu_custom_call" | custom-call | tf_op jit(solution)/shard_map/pallas_call | solution.py:718
  164.2 2.6 %shard_map.131 = (bf16[768,128]{1,0:T(8,128)(2,1)}, f32[8,128,128]{2,1,0:T(8,128)}, f32[8,128,128]{2,1,0:T(8,128)}) custom-call(s32[8]{0:T(128)} %step_of.3, f32[1,128]{1,0:T(1,128)} %bitcast.13, bf16[768,128]{1,0:T(8,128)(2,1)} %get-tuple-element.9.raw, f32[8,128,128]{2,1,0:T(8,128)} %bitcast.10, f32[16,128]{1,0:T(8,128)} %get-tuple-element.11.touched, ...), custom_call_target="tpu_custom_call" | custom-call | tf_op jit(solution)/shard_map/pallas_call | solution.py:744
  (3 shorter events, 0.0 us)
Async XLA Ops:
  0.6 0.7 copy-start.1
  1.5 0.5 copy-start

commit v4 on v3

--- a/solution.py
+++ b/solution.py
@@ -31,7 +31,8 @@
 TSTART = 3
 TPACE = ()
 CSTART = 8
-CPACE = (3,)
+CPACE = (4,)
+SETTLE = 4
 MESH = pl.DeviceIdType.MESH
 HOPS = ((8, 7), (7, 8))
 VM = pl.BlockSpec(memory_space=pltpu.VMEM)
@@ -674,9 +675,10 @@
 
 def settle_kernel(step_of, rate, raw, total, touched, values, momentum, out, new_values, new_momentum):
     out[...] = raw[...]
-    for p in range(LOCAL):
-        f = jnp.exp(-(STEP - step_of[p]).astype(F32) * rate[...])
-        hit = touched[p : p + 1, :] > 0.5
+    for p in range(LOCAL // SETTLE):
+        page = pl.program_id(0) * (LOCAL // SETTLE) + p
+        f = jnp.exp(-(STEP - step_of[page]).astype(F32) * rate[...])
+        hit = touched[pl.ds(page, 1), :] > 0.5
         v, m = values[p], momentum[p]
         m = jnp.where(hit, MOMENTUM_RATE * m + total[p] * f, m)
         new_momentum[p] = m
@@ -741,6 +743,8 @@
         gate_weight,
         out_weight,
     )
+    rows = pl.BlockSpec((ROWS // SETTLE, LANE), lambda i: (i, 0))
+    pages = pl.BlockSpec((LOCAL // SETTLE, PAGE, LANE), lambda i: (i, 0, 0))
     layer_out, new_values, new_momentum = pl.pallas_call(
         settle_kernel,
         out_shape=(
@@ -748,8 +752,9 @@
             jax.ShapeDtypeStruct(paged, F32),
             jax.ShapeDtypeStruct(paged, F32),
         ),
-        in_specs=[SM] + [VM] * 6,
-        out_specs=(VM,) * 3,
+        grid=(SETTLE,),
+        in_specs=[SM, VM, rows, pages, VM, pages, pages],
+        out_specs=(rows, pages, pages),
     )(last_step, rate, raw, total.reshape(paged), touched, stored, momentum.reshape(paged))
     return (layer_out, new_values.reshape(OWN, LANE), new_momentum.reshape(OWN, LANE))
 

time: 167 us -> 168 us (level)
  no operation moved by 1% of the time
where the time goes in v4:
time: 168 us; the launch traced here: 167 us
  Pallas kernels  164 us (98%)
    pallas_call x1, Pallas kernels, per_device(): pl.pallas_call(kernel, out_shape=(jax.ShapeDtypeStruct((ROWS, LANE), BF16...  160 us
    pallas_call x1, Pallas kernels, per_device(): pl.pallas_call(settle_kernel, out_shape=(jax.ShapeDtypeStruct((ROWS, LANE...  3.66 us

profile of v4, /device:TPU:1, one launch (start us, length us, event | category | flops | bytes accessed | tf_op | source)
XLA Modules:
  0.0 167.3 jit_solution(18167720312756598345)
XLA Ops:
  0.6 0.0 copy-start.1
  0.7 0.7 copy-done.1
  1.3 0.1 copy.16
  1.4 0.1 reshape.111.pids
  1.5 0.0 copy-start
  1.5 0.5 copy-done
  2.0 0.1 fusion.3
  2.1 0.5 and_select_fusion
  2.6 0.1 fusion.1
  2.7 0.6 and_convert_fusion.mark
  3.3 160.2 %shard_map.130 = (bf16[768,128]{1,0:T(8,128)(2,1)}, f32[1024,128]{1,0:T(8,128)}, f32[16,128]{1,0:T(8,128)}) custom-call(s32[48]{0:T(128)} %copy-done, s32[64]{0:T(128)} %get-tuple-element.20.pair, s32[64]{0:T(128)} %get-tuple-element.19.block, f32[512]{0:T(512)} %and_convert_fusion.mark, s32[8]{0:T(128)} %step_of.3, bf16[8,128,128]{2,1,0:T(8,128)(2,1)} %bitcast.11, ...), custom_call_target="tpu_custom_call" | custom-call | tf_op jit(solution)/shard_map/pallas_call | solution.py:720
  163.6 3.7 %shard_map.131 = (bf16[768,128]{1,0:T(8,128)(2,1)}, f32[8,128,128]{2,1,0:T(8,128)}, f32[8,128,128]{2,1,0:T(8,128)}) custom-call(s32[8]{0:T(128)} %step_of.3, f32[1,128]{1,0:T(1,128)} %bitcast.13, bf16[768,128]{1,0:T(8,128)(2,1)} %get-tuple-element.9.raw, f32[8,128,128]{2,1,0:T(8,128)} %bitcast.10, f32[16,128]{1,0:T(8,128)} %get-tuple-element.11.touched, ...), custom_call_target="tpu_custom_call" | custom-call | tf_op jit(solution)/shard_map/pallas_call | solution.py:748
  (3 shorter events, 0.0 us)
Async XLA Ops:
  0.6 0.7 copy-start.1
  1.5 0.5 copy-start
